TPU v7x, 512 devices: a whole 4x8x8 slice. The times are simulated.
512 devices in a mesh: dp: 4 (over x), node: 16 (over z, core), expert: 8 (over y).
Axes of the slice: x: 4, y: 8, z: 8, core: 2. Of those that a mesh axis runs over, the one named last changes fastest.
Arguments:
- x_rollout: bfloat16 [8192, 4096], P(('dp', 'node'), 'expert'), may hold values from -6 to 6
- dest: int32 [8192], P(('dp', 'node')), may hold values from 0 to 8191, as said below
- route_ids: int32 [8192, 4], P(('dp', 'node')), may hold values from 0 to 127, as said below
- route_weights: float32 [8192, 4], P(('dp', 'node')), may hold values from 0.2 to 1
- cotangent: bfloat16 [8192, 4096], P(('dp', 'node'), 'expert'), may hold values from -0.59765625 to 0.59765625
- w_up: bfloat16 [128, 1024, 4096], P(('node', 'expert'), 'dp'), may hold values from -0.09375 to 0.09375
- w_down: bfloat16 [128, 1024, 4096], P(('node', 'expert'), 'dp'), may hold values from -0.1875 to 0.1875
Outputs:
- grad_tokens: bfloat16 [8192, 4096], P(('dp', 'node'), 'expert')
- grad_weights: bfloat16 [8192, 4], P(('dp', 'node'))
Inputs may be any that keep to these rules, and one draw needn't show every extreme that they name: `dest`: A permutation of the 8192 rows. Learner shard (d, n) holds rows (d * 16 + n) * 128 to (d * 16 + n) * 128 + 127, and rollout shards are laid out alike. A row of rollout shard (s, n) goes to some learner shard (d, n) of the same n, at a position p within that shard with p mod 4 = s. `route_ids`: each row names 4 different experts, two in each of 2 node groups, listed group by group; expert k lies in node group k // 8. The two groups of a row of learner shard (d, n) are n + o and n + o + 8, modulo 16, for an offset o from 0 to 7 of that row; the two experts of a row in one group lie 4 apart modulo 8. Among the rows of one learner shard at most 24 use any one node group and at most 6 name any one expert; in every shard some node group is used by exactly 24 rows and some expert is named by exactly 6.
All inputs are finite; a program needn't handle non-finite values.
Results may differ from a plain program's by a relative error of at most 0.015.
Values may be sent and summed in bfloat16 or wider, within the bound.
No kernel may reach another device: no remote copies, remote signals or barrier semaphores. Data moves between devices by JAX's collectives and lax.ppermute only.
A program may use at most 64 MiB of HBM per device.

v0:
```python
import jax
import jax.numpy as jnp
from jax import lax
from jax.sharding import PartitionSpec as P


def rank_slots(labels, label_total):
    matches = labels[..., None] == jnp.arange(label_total, dtype=jnp.int32)
    used_rows = jnp.any(matches, axis=1).astype(jnp.int32)
    before = jnp.cumsum(used_rows, axis=0) - used_rows
    return jnp.sum(jnp.where(matches, before[:, None, :], 0), axis=2)


def pack_rows(values, index, repeat_count, slots):
    spread = jnp.repeat(values, repeat_count, axis=0)
    empty = jnp.zeros((slots,) + values.shape[1:], values.dtype)
    return empty.at[index].set(spread, mode="drop")


def block_terms(rows_x, rows_dy, up_rows, down_rows):
    pre_act = jnp.einsum("rd,hd->rh", rows_x, up_rows, preferred_element_type=jnp.float32)
    grad_hidden = jnp.einsum("rd,hd->rh", rows_dy, down_rows, preferred_element_type=jnp.float32)
    gate_sig = jax.nn.sigmoid(pre_act)
    scores = jnp.sum(pre_act * gate_sig * grad_hidden, axis=1)
    grad_pre = (grad_hidden * gate_sig * (1.0 + pre_act * (1.0 - gate_sig))).astype(jnp.bfloat16)
    return (grad_pre, scores)


def shards(x_rollout, dest, route_ids, route_weights, cotangent, w_up, w_down):
    dp_size = lax.axis_size("dp")
    node_size = lax.axis_size("node")
    group_size = lax.axis_size("expert")
    tok_rows, width_part = x_rollout.shape
    route_count = route_ids.shape[1]
    group_count = route_count // 2
    group_step = node_size // group_count
    group_cap = 3 * tok_rows // (2 * group_step)
    expert_cap = 2 * group_cap // group_size
    share_rows = tok_rows // dp_size
    expert_total = node_size * group_size
    full_width = width_part * group_size
    target_shard = dest // (node_size * tok_rows)
    sort_order = jnp.argsort(target_shard * tok_rows + dest % tok_rows)
    outgoing = x_rollout[sort_order].reshape(dp_size, share_rows, width_part)
    arrived = lax.all_to_all(outgoing, "dp", split_axis=0, concat_axis=0, tiled=True)
    tokens = jnp.transpose(arrived, (1, 0, 2)).reshape(tok_rows, width_part)
    route_slot = rank_slots(route_ids, expert_total)
    flat_index = (route_ids * expert_cap + route_slot).reshape(-1)
    send_x = pack_rows(tokens, flat_index, route_count, expert_total * expert_cap)
    send_dy = pack_rows(cotangent, flat_index, route_count, expert_total * expert_cap)
    got_x, got_dy = (
        lax.all_to_all(
            lax.all_to_all(
                send_x.reshape(node_size, group_size, expert_cap, width_part),
                "node",
                split_axis=0,
                concat_axis=0,
                tiled=True,
            ),
            "expert",
            split_axis=1,
            concat_axis=3,
            tiled=True,
        ),
        lax.all_to_all(
            lax.all_to_all(
                send_dy.reshape(node_size, group_size, expert_cap, width_part),
                "node",
                split_axis=0,
                concat_axis=0,
                tiled=True,
            ),
            "expert",
            split_axis=1,
            concat_axis=3,
            tiled=True,
        ),
    )
    rows_x = got_x.reshape(node_size * expert_cap, full_width)
    rows_dy = got_dy.reshape(node_size * expert_cap, full_width)
    up_rows = w_up[0]
    down_rows = w_down[0]
    all_x, all_dy = (
        lax.all_gather(rows_x, "dp", axis=0, tiled=True),
        lax.all_gather(rows_dy, "dp", axis=0, tiled=True),
    )
    grad_pre, score_part = block_terms(all_x, all_dy, up_rows, down_rows)
    summed = lax.psum_scatter(
        jnp.dot(grad_pre, up_rows, preferred_element_type=jnp.float32).astype(jnp.bfloat16),
        "dp",
        scatter_dimension=0,
        tiled=True,
    )
    scores = lax.psum_scatter(score_part, "dp", scatter_dimension=0, tiled=True)
    back_rows = summed.reshape(node_size, expert_cap, group_size, width_part)
    back_scores = jnp.broadcast_to(
        scores.astype(jnp.bfloat16).reshape(node_size, expert_cap, 1),
        (node_size, expert_cap, group_size),
    )
    ret_rows, ret_scores = (
        lax.all_to_all(
            lax.all_to_all(back_rows, "node", split_axis=0, concat_axis=0, tiled=True),
            "expert",
            split_axis=2,
            concat_axis=2,
            tiled=True,
        ),
        lax.all_to_all(
            lax.all_to_all(back_scores, "node", split_axis=0, concat_axis=0, tiled=True),
            "expert",
            split_axis=2,
            concat_axis=2,
            tiled=True,
        ),
    )
    pick_index = (
        (route_ids // group_size * expert_cap + route_slot) * group_size + route_ids % group_size
    ).reshape(-1)
    chosen = ret_rows.reshape(-1, width_part)[pick_index].reshape(tok_rows, route_count, width_part)
    grad_tokens = jnp.sum(route_weights[:, :, None] * chosen.astype(jnp.float32), axis=1)
    grad_weights = ret_scores.reshape(-1)[pick_index].reshape(tok_rows, route_count)
    return (grad_tokens.astype(jnp.bfloat16), grad_weights)


def solution(mesh):
    in_specs = (
        P(("dp", "node"), "expert"),
        P(("dp", "node")),
        P(("dp", "node"), None),
        P(("dp", "node"), None),
        P(("dp", "node"), "expert"),
        P(("node", "expert"), "dp", None),
        P(("node", "expert"), "dp", None),
    )
    out_specs = (P(("dp", "node"), "expert"), P(("dp", "node"), None))
    return jax.shard_map(shards, mesh=mesh, in_specs=in_specs, out_specs=out_specs, check_vma=False)
```

profile of v0, /device:TPU:1, one launch (start us, length us, event | category | flops | bytes accessed | tf_op | source)
XLA Modules:
  0.0 327.6 jit_solution(16552685546476685811)
XLA Ops:
  8.0 2.5 sort.17
  10.5 2.5 gather_fusion
  13.0 4.8 %all-to-all-start.2 = ((bf16[4,32,512]{2,1,0:T(8,128)(2,1)}), bf16[4,32,512]{2,1,0:T(8,128)(2,1)S(1)}, u32[]{:S(2)}, u32[]{:S(2)}) async-start(bf16[4,32,512]{2,1,0:T(8,128)(2,1)} %bitcast.4), calls=%async_computation.2 | async-start | bytes 262144 | tf_op jit(solution)/shard_map/all_to_all | solution.py:45
  23.1 3.3 %scatter_custom_fusion.1 = bf16[768,512]{1,0:T(8,128)(2,1)} fusion(s32[512]{0:T(512)S(1)} %bitcast.46, bf16[512,512]{1,0:T(8,128)(2,1)S(1)} %reshape.174, bf16[]{:T(256)} %constant.59.clone.1), kind=kCustom, calls=%fused_computation.15 | custom fusion | bytes 786434 | tf_op jit(solution)/shard_map/scatter | solution.py:17
  28.0 35.2 %all_to_all.65 = bf16[16,8,6,512]{3,1,2,0:T(8,128)(2,1)S(1)} all-to-all(bf16[16,8,6,512]{3,1,2,0:T(8,128)(2,1)S(1)} %copy.57), channel_id=1, replica_groups=mesh['dp'=4,'node'=16,'expert'=8] {'node'}, dimensions={0} | all-to-all | bytes 1572864 | tf_op jit(solution)/shard_map/all_to_all | solution.py:53
  63.7 30.4 %all_to_all.66 = bf16[16,8,6,512]{3,0,2,1:T(8,128)(2,1)S(1)} all-to-all(bf16[16,8,6,512]{3,0,2,1:T(8,128)(2,1)S(1)} %copy.58), channel_id=1, replica_groups=mesh['dp'=4,'node'=16,'expert'=8] {'expert'}, dimensions={1} | all-to-all | bytes 1572864 | tf_op jit(solution)/shard_map/all_to_all | solution.py:52
  96.0 3.3 %scatter_custom_fusion = bf16[768,512]{1,0:T(8,128)(2,1)} fusion(s32[512]{0:T(512)S(1)} %bitcast.47, bf16[512,512]{1,0:T(8,128)(2,1)S(1)} %reshape.166, bf16[]{:T(256)} %constant.59.clone.1), kind=kCustom, calls=%fused_computation.17 | custom fusion | bytes 786434 | tf_op jit(solution)/shard_map/scatter | solution.py:17
  101.0 26.0 %all_to_all.67 = bf16[16,8,6,512]{3,1,2,0:T(8,128)(2,1)S(1)} all-to-all(bf16[16,8,6,512]{3,1,2,0:T(8,128)(2,1)S(1)} %copy.53), channel_id=1, replica_groups=mesh['dp'=4,'node'=16,'expert'=8] {'node'}, dimensions={0} | all-to-all | bytes 1572864 | tf_op jit(solution)/shard_map/all_to_all | solution.py:66
  127.4 25.8 %all_to_all.68 = bf16[16,8,6,512]{3,0,2,1:T(8,128)(2,1)S(1)} all-to-all(bf16[16,8,6,512]{3,0,2,1:T(8,128)(2,1)S(1)} %copy.54), channel_id=1, replica_groups=mesh['dp'=4,'node'=16,'expert'=8] {'expert'}, dimensions={1} | all-to-all | bytes 1572864 | tf_op jit(solution)/shard_map/all_to_all | solution.py:65
  155.1 3.2 fusion.1
  158.3 31.3 %all-gather.3.cloned.1.call-done = bf16[384,4096]{1,0:T(8,128)(2,1)} async-done(((bf16[96,4096]{1,0:T(8,128)(2,1)}), bf16[384,4096]{1,0:T(8,128)(2,1)}) %all-gather.3.cloned.1.call-update) | async-done | bytes 3145744 | tf_op jit(solution)/shard_map/all_gather | solution.py:85
  189.5 3.8 %multiply_reduce_fusion.1 = (f32[384]{0:T(512)S(1)}, f32[384,256]{0,1:T(8,128)S(1)}) fusion(f32[384,256]{0,1:T(8,128)S(1)} %fusion.1, bf16[384,4096]{1,0:T(8,128)(2,1)} %all-gather.3.cloned.1.call-done, bf16[1,256,4096]{2,1,0:T(8,128)(2,1)} %param.13), kind=kOutput, calls=%fused_computation.12 | convolution fusion | flops 805895808 | bytes 6030848 | tf_op jit(solution)/shard_map/rd,hd->rh/dot_general | solution.py:22
  193.4 2.8 convolution_convert_fusion
  198.1 6.6 %all-reduce = bf16[384]{0:T(512)(128)(2,1)S(1)} all-reduce(f32[384]{0:T(512)S(1)} %get-tuple-element.14), channel_id=3, replica_groups=mesh['dp'=4,'node'=16,'expert'=8] {'dp'}, use_global_device_ids=true, to_apply=%region_9.10.clone | all-reduce | flops 384 | bytes 2304
  205.5 10.2 %all-to-all-start.7 = ((bf16[16,6,8]{1,2,0:T(8,128)(2,1)}), bf16[16,6,8]{1,2,0:T(8,128)(2,1)S(1)}, u32[]{:S(2)}, u32[]{:S(2)}) async-start(bf16[16,6,8]{1,2,0:T(8,128)(2,1)} %broadcast_in_dim.42), calls=%async_computation.8 | async-start | bytes 65536 | tf_op jit(solution)/shard_map/all_to_all | solution.py:109
  215.7 24.5 %reduce-scatter.2.cloned.1.call-done = bf16[96,4096]{1,0:T(8,128)(2,1)} async-done(((bf16[384,4096]{1,0:T(8,128)(2,1)}), bf16[96,4096]{1,0:T(8,128)(2,1)}) %reduce-scatter.2.cloned.1.call-update) | async-done | bytes 786448 | tf_op jit(solution)/shard_map/reduce_scatter | solution.py:88
  242.5 8.0 %all-to-all-start.5 = ((bf16[16,6,8,512]{3,2,1,0:T(8,128)(2,1)}), bf16[16,6,8,512]{3,2,1,0:T(8,128)(2,1)S(1)}, u32[]{:S(2)}, u32[]{:S(2)}) async-start(bf16[16,6,8,512]{3,2,1,0:T(8,128)(2,1)} %bitcast.38), calls=%async_computation.6 | async-start | bytes 1572864 | tf_op jit(solution)/shard_map/all_to_all | solution.py:102
  251.2 21.9 %all-to-all-done.5 = bf16[16,6,8,512]{3,2,1,0:T(8,128)(2,1)S(1)} async-done(((bf16[16,6,8,512]{3,2,1,0:T(8,128)(2,1)}), bf16[16,6,8,512]{3,2,1,0:T(8,128)(2,1)S(1)}, u32[]{:S(2)}, u32[]{:S(2)}) %all-to-all-start.5) | async-done | bytes 786464 | tf_op jit(solution)/shard_map/all_to_all | solution.py:102
  273.2 6.5 %all-to-all-start.8 = ((bf16[16,6,8]{0,1,2:T(8,128)(2,1)}), bf16[16,6,8]{0,1,2:T(8,128)(2,1)S(1)}, u32[]{:S(2)}, u32[]{:S(2)}) async-start(bf16[16,6,8]{0,1,2:T(8,128)(2,1)} %copy.63), calls=%async_computation.9 | async-start | bytes 32768 | tf_op jit(solution)/shard_map/all_to_all | solution.py:108
  281.0 5.3 %all-to-all-done.8 = bf16[16,6,8]{0,1,2:T(8,128)(2,1)S(1)} async-done(((bf16[16,6,8]{0,1,2:T(8,128)(2,1)}), bf16[16,6,8]{0,1,2:T(8,128)(2,1)S(1)}, u32[]{:S(2)}, u32[]{:S(2)}) %all-to-all-start.8) | async-done | bytes 1568 | tf_op jit(solution)/shard_map/all_to_all | solution.py:108
  286.2 4.2 %all-to-all-start.6 = ((bf16[16,6,8,512]{3,0,1,2:T(8,128)(2,1)}), bf16[16,6,8,512]{3,0,1,2:T(8,128)(2,1)}, u32[]{:S(2)}, u32[]{:S(2)}) async-start(bf16[16,6,8,512]{3,0,1,2:T(8,128)(2,1)} %copy.60), calls=%async_computation.7 | async-start | bytes 1572864 | tf_op jit(solution)/shard_map/all_to_all | solution.py:101
  291.0 3.5 %gather_fusion.2 = bf16[512]{0:T(512)(128)(2,1)S(1)} fusion(bf16[768]{0:T(1024)(128)(2,1)S(1)} %reshape.135, s32[1024]{0:T(1024)S(1)} %pad_clamp_fusion), kind=kCustom, calls=%fused_computation.2 | custom fusion | bytes 4096 | tf_op jit(solution)/shard_map/gather | solution.py:121
  295.3 18.8 %all-to-all-done.6 = bf16[16,6,8,512]{3,0,1,2:T(8,128)(2,1)} async-done(((bf16[16,6,8,512]{3,0,1,2:T(8,128)(2,1)}), bf16[16,6,8,512]{3,0,1,2:T(8,128)(2,1)}, u32[]{:S(2)}, u32[]{:S(2)}) %all-to-all-start.6) | async-done | bytes 786464 | tf_op jit(solution)/shard_map/all_to_all | solution.py:101
  315.7 2.6 gather_fusion.1
  (63 shorter events, 26.1 us)
Async XLA Ops:
  7.2 147.9 %copy-start = (bf16[1,256,4096]{2,1,0:T(8,128)(2,1)S(1)}, bf16[1,256,4096]{2,1,0:T(8,128)(2,1)}, u32[]{:S(2)}) copy-start(bf16[1,256,4096]{2,1,0:T(8,128)(2,1)} %param.12) | copy-start | bytes 6291460
  13.0 9.7 %all-to-all-start.2 = ((bf16[4,32,512]{2,1,0:T(8,128)(2,1)}), bf16[4,32,512]{2,1,0:T(8,128)(2,1)S(1)}, u32[]{:S(2)}, u32[]{:S(2)}) async-start(bf16[4,32,512]{2,1,0:T(8,128)(2,1)} %bitcast.4), calls=%async_computation.2 | async-start | bytes 262144 | tf_op jit(solution)/shard_map/all_to_all | solution.py:45
  17.8 137.3 %all-gather.5.cloned.1.call-start = ((), (), s32[]{:S(2)}) async-start(), calls=%async_computation.11 | async-start | bytes 3932160 | tf_op jit(solution)/shard_map/all_gather | solution.py:84
  63.6 32.1 %copy-start.1 = (bf16[128,512]{1,0:T(8,128)(2,1)S(1)}, bf16[128,512]{1,0:T(8,128)(2,1)}, u32[]{:S(2)}) copy-start(bf16[128,512]{1,0:T(8,128)(2,1)} %param.11) | copy-start | bytes 393220
  95.7 93.8 %all-gather.3.cloned.1.call-start = ((), (), s32[]{:S(2)}) async-start(), calls=%async_computation.10 | async-start | bytes 3932160 | tf_op jit(solution)/shard_map/all_gather | solution.py:85
  154.8 85.3 %reduce-scatter.2.cloned.1.call-start = ((), (), s32[]{:S(2)}) async-start(), calls=%async_computation.12 | async-start | bytes 3932160 | tf_op jit(solution)/shard_map/reduce_scatter | solution.py:88
  205.5 37.0 %all-to-all-start.7 = ((bf16[16,6,8]{1,2,0:T(8,128)(2,1)}), bf16[16,6,8]{1,2,0:T(8,128)(2,1)S(1)}, u32[]{:S(2)}, u32[]{:S(2)}) async-start(bf16[16,6,8]{1,2,0:T(8,128)(2,1)} %broadcast_in_dim.42), calls=%async_computation.8 | async-start | bytes 65536 | tf_op jit(solution)/shard_map/all_to_all | solution.py:109
  240.2 50.5 %copy-start.2 = (f32[128,4]{0,1:T(4,128)S(1)}, f32[128,4]{0,1:T(4,128)}, u32[]{:S(2)}) copy-start(f32[128,4]{0,1:T(4,128)} %param.10) | copy-start | bytes 6148
  242.5 30.7 %all-to-all-start.5 = ((bf16[16,6,8,512]{3,2,1,0:T(8,128)(2,1)}), bf16[16,6,8,512]{3,2,1,0:T(8,128)(2,1)S(1)}, u32[]{:S(2)}, u32[]{:S(2)}) async-start(bf16[16,6,8,512]{3,2,1,0:T(8,128)(2,1)} %bitcast.38), calls=%async_computation.6 | async-start | bytes 1572864 | tf_op jit(solution)/shard_map/all_to_all | solution.py:102
  273.2 13.1 %all-to-all-start.8 = ((bf16[16,6,8]{0,1,2:T(8,128)(2,1)}), bf16[16,6,8]{0,1,2:T(8,128)(2,1)S(1)}, u32[]{:S(2)}, u32[]{:S(2)}) async-start(bf16[16,6,8]{0,1,2:T(8,128)(2,1)} %copy.63), calls=%async_computation.9 | async-start | bytes 32768 | tf_op jit(solution)/shard_map/all_to_all | solution.py:108
  286.2 27.9 %all-to-all-start.6 = ((bf16[16,6,8,512]{3,0,1,2:T(8,128)(2,1)}), bf16[16,6,8,512]{3,0,1,2:T(8,128)(2,1)}, u32[]{:S(2)}, u32[]{:S(2)}) async-start(bf16[16,6,8,512]{3,0,1,2:T(8,128)(2,1)} %copy.60), calls=%async_computation.7 | async-start | bytes 1572864 | tf_op jit(solution)/shard_map/all_to_all | solution.py:101
Sparse Core Ops, SparseCore 0:
  95.8 34.3 all-gather.4
  155.0 34.5 all-gather.2
  196.3 43.8 reduce-scatter.1
where the time goes:
time: 329 us; the launch traced here: 328 us
  blocking collectives  124 us (38%)
  waiting for transfers between devices  104 us (32%)
  local copies, waits for them, and re-layouts  34.2 us (10%)
  starting transfers between devices  34 us (10%)
  between operations  14.6 us (4%)
  matrix products  9.75 us (3%)
  other arithmetic  7.37 us (2%)
    all_to_all x1, blocking collectives, shards(): lax.all_to_all(send_x.reshape(node_size, group_size, expert_cap, width_pa...  35.2 us
    all_gather x1, waiting for transfers between devices, shards(): lax.all_gather(rows_dy, 'dp', axis=0, tiled=True)  31.3 us
    all_to_all x1, blocking collectives, shards(): lax.all_to_all(lax.all_to_all(send_x.reshape(node_size, group_size, exper...  30.4 us
    all_to_all x1, blocking collectives, shards(): lax.all_to_all(send_dy.reshape(node_size, group_size, expert_cap, width_p...  26 us
    all_to_all x1, blocking collectives, shards(): lax.all_to_all(lax.all_to_all(send_dy.reshape(node_size, group_size, expe...  25.8 us
    reduce_scatter x1, waiting for transfers between devices, shards(): lax.psum_scatter(jnp.dot(grad_pre, up_rows, preferred_element_type=jnp.fl...  24.5 us
    all_to_all x1, waiting for transfers between devices, shards(): lax.all_to_all(back_rows, 'node', split_axis=0, concat_axis=0, tiled=True)  21.9 us
    all_to_all x1, waiting for transfers between devices, shards(): lax.all_to_all(lax.all_to_all(back_rows, 'node', split_axis=0, concat_axi...  18.8 us
  transfers between devices with their start and end apart: 8, of which 6 were waited for; matrix products, arithmetic and copies ran while one was open for 7% of the time, Pallas kernels for 0%

commit v1 on v0

v1 whole, which is shorter than its diff:
```python
import functools

import jax
import jax.numpy as jnp
import numpy as np
from jax import lax
from jax.experimental import pallas as pl
from jax.experimental.pallas import tpu as pltpu
from jax.sharding import PartitionSpec as P

BF = jnp.bfloat16
F32 = jnp.float32
CAP = 6
TOK = 128
WID = 512
LANE = 128
PARAMS = pltpu.CompilerParams(vmem_limit_bytes=32 * 1024 * 1024)


def np_pack():
    m = np.zeros((384, 384), np.float32)
    for k in range(8):
        for a in range(8):
            for s in range(6):
                m[k * 48 + a * 6 + s, a * 48 + s * 8 + k] = 1
    return m


def np_unpack():
    m = np.zeros((384, 384), np.float32)
    for n in range(8):
        for a in range(8):
            for s in range(6):
                m[a * 48 + n * 6 + s, n * 48 + a * 6 + s] = 1
    return m


def np_reply():
    m = np.zeros((256, 256), np.float32)
    for n in range(8):
        for s in range(6):
            for c in range(4):
                m[n * 32 + c * 6 + s, c * 48 + n * 6 + s] = 1
            m[n * 32 + 24, 192 + n * 6 + s] = 1
    return m


def np_collect():
    m = np.zeros((208, 256), np.float32)
    for k in range(8):
        for c in range(4):
            for s in range(6):
                m[c * 48 + k * 6 + s, k * 32 + c * 6 + s] = 1
        m[192 + k, k * 32 + 24] = 1
    return m


def np_slot_mask():
    m = np.zeros((96, LANE), np.float32)
    for r in range(96):
        m[r, r % 6] = 1
    return m


def iota(shape, dim):
    return lax.broadcasted_iota(jnp.int32, shape, dim)


def dot(a, b):
    return jnp.dot(a, b, preferred_element_type=F32)


def dot_nt(a, b):
    return lax.dot_general(a, b, (((1,), (1,)), ((), ())), preferred_element_type=F32)


def dot_tn(a, b):
    return lax.dot_general(a, b, (((0,), (0,)), ((), ())), preferred_element_type=F32)


def named_by(info):
    experts = iota((TOK, LANE), 1).astype(F32)
    named = jnp.zeros((TOK, LANE), F32)
    for j in range(4):
        named = named + jnp.where(info[:, j:j + 1] == experts, 1.0, 0.0)
    return named


def prepare_kernel(shard_step, x_ref, dest_ref, dy_ref, ids_ref, w_ref, sorted_ref, pay_ref):
    dest = dest_ref[...]
    target = (dest // shard_step) * 32 + (dest % TOK) // 4
    pick = jnp.where(iota((TOK, TOK), 0) == target, 1.0, 0.0).astype(BF)
    sorted_ref[...] = dot(pick, x_ref[...]).astype(BF)
    pay_ref[:, :WID] = dy_ref[...]
    lanes = iota((TOK, LANE), 1)
    info = jnp.zeros((TOK, LANE), F32)
    ids = ids_ref[...].astype(F32)
    weights = w_ref[...]
    for j in range(4):
        info = jnp.where(lanes == j, ids[:, j:j + 1], info)
        rest = weights[:, j:j + 1]
        for piece in range(3):
            part = rest.astype(BF).astype(F32)
            info = jnp.where(lanes == 4 + 4 * piece + j, part, info)
            rest = rest - part
    pay_ref[:, WID:] = info.astype(BF)


def pack_kernel(pay_ref, x_ref, perm_ref, out_ref, slots, rows):
    info = pay_ref[:, WID:].astype(F32)
    named = named_by(info).astype(BF)
    earlier = jnp.where(iota((TOK, TOK), 0) < iota((TOK, TOK), 1), 1.0, 0.0).astype(BF)
    same = jnp.where(iota((TOK, TOK), 0) == iota((TOK, TOK), 1), 1.0, 0.0).astype(BF)
    rank = dot_tn(named, earlier)
    named_t = dot_tn(named, same)
    for s in range(CAP):
        slots[s] = jnp.where(rank == float(s), named_t, 0.0)
    token = iota((TOK, TOK), 0)
    order = jnp.where(iota((TOK, TOK), 1) == (token % 4) * 32 + token // 4, 1.0, 0.0).astype(BF)
    rows[:, :WID] = pay_ref[:, :WID]
    rows[:, WID:] = dot(order, x_ref[...]).astype(BF)
    perm = perm_ref[...]
    for pair in range(8):
        halves = []
        for block in (2 * pair, 2 * pair + 1):
            pick = jnp.concatenate([slots[s, block * 8:block * 8 + 8, :] for s in range(CAP)], axis=0).astype(BF)
            got = dot(pick, rows[...]).astype(BF)
            halves.append(jnp.concatenate([got[:, a * LANE:(a + 1) * LANE] for a in range(8)], axis=0))
        sent = dot(perm, jnp.concatenate(halves, axis=1)).astype(BF)
        for h in range(2):
            out_ref[(2 * pair + h) * 8:(2 * pair + h) * 8 + 8] = sent[:, h * LANE:(h + 1) * LANE].reshape(8, 48, LANE)


def forward_kernel(me_ref, got_ref, w0, w1, w2, w3, perm_ref, out_ref, dy_rows, x_rows):
    perm = perm_ref[...]
    for d in range(4):
        for half in range(2):
            base = d * 96 + half * 48
            both = jnp.concatenate(
                [got_ref[half * 8:half * 8 + 8, 2 * d + b].reshape(384, LANE) for b in range(2)], axis=1
            )
            moved = dot(perm, both).astype(BF)
            for a in range(8):
                target = dy_rows if a < 4 else x_rows
                for b in range(2):
                    col = (b * 4 + a % 4) * LANE
                    target[base:base + 48, col:col + LANE] = moved[a * 48:a * 48 + 48, b * LANE:(b + 1) * LANE]
    me = me_ref[0]
    for k, w in enumerate((w0, w1, w2, w3)):
        block = lax.rem(me - k + 4, 4)
        pre = dot_nt(x_rows[...], w[:256]).astype(BF)
        grad = dot_nt(dy_rows[...], w[256:]).astype(BF)
        out_ref[:, block, :, :256] = pre.reshape(4, 96, 256)
        out_ref[:, block, :, 256:] = grad.reshape(4, 96, 256)


def act_kernel(part_ref, mask_ref, out_ref):
    score = jnp.zeros((96, 1), F32)
    for block in range(4):
        total = part_ref[0, block].astype(F32)
        for s in range(1, 4):
            total = total + part_ref[s, block].astype(F32)
        pre = total[:, :256]
        grad = total[:, 256:]
        sig = jax.nn.sigmoid(pre)
        score = score + jnp.sum(pre * sig * grad, axis=1, keepdims=True)
        out_ref[:, block * 256:block * 256 + 256] = (grad * sig * (1.0 + pre * (1.0 - sig))).astype(BF)
    out_ref[:, 1024:] = (score * mask_ref[...].astype(F32)).astype(BF)


def backward_kernel(me_ref, grad_ref, w0, w1, w2, w3, perm_ref, out_ref, rows):
    me = me_ref[0]
    total = jnp.zeros((384, 1024), F32)
    for k, w in enumerate((w0, w1, w2, w3)):
        block = lax.rem(me - k + 4, 4)
        part = grad_ref[:, :, pl.ds(pl.multiple_of(block * 256, 256), 256)].reshape(384, 256)
        total = total + dot(part, w[...])
    rows[...] = total.astype(BF)
    perm = perm_ref[...]
    for d in range(4):
        for half in range(2):
            base = d * 96 + half * 48
            score = grad_ref[d, half * 48:half * 48 + 48, 1024:]
            stacks = []
            for b in range(2):
                parts = [rows[base:base + 48, (b * 4 + c) * LANE:(b * 4 + c + 1) * LANE] for c in range(4)]
                stacks.append(jnp.concatenate(parts + [score, jnp.zeros((16, LANE), BF)], axis=0))
            sent = dot(perm, jnp.concatenate(stacks, axis=1)).astype(BF)
            for b in range(2):
                out_ref[half * 8:half * 8 + 8, 2 * d + b] = sent[:, b * LANE:(b + 1) * LANE].reshape(8, 32, LANE)


def combine_kernel(got_ref, info_ref, perm_ref, out_ref, rows, scores):
    info = info_ref[...].astype(F32)
    named = named_by(info).astype(BF)
    later = jnp.where(iota((TOK, TOK), 1) < iota((TOK, TOK), 0), 1.0, 0.0).astype(BF)
    rank = dot(later, named)
    perm = perm_ref[...]
    for pair in range(8):
        both = jnp.concatenate(
            [got_ref[(2 * pair + h) * 8:(2 * pair + h) * 8 + 8].reshape(256, LANE) for h in range(2)], axis=1
        )
        moved = dot(perm, both)
        for h in range(2):
            block = 2 * pair + h
            half = moved[:, h * LANE:(h + 1) * LANE]
            scores[block * 8:block * 8 + 8] = half[192:200]
            for c in range(4):
                rows[block * 48:block * 48 + 48, c * LANE:(c + 1) * LANE] = half[c * 48:c * 48 + 48].astype(BF)
    lanes = iota((TOK, LANE), 1).astype(F32)
    wide = iota((TOK, 128 * CAP), 1).astype(F32)
    coefs = [jnp.zeros((TOK, 128 * CAP), F32) for _ in range(3)]
    table = scores[...].astype(BF)
    back = jnp.zeros((TOK, LANE), F32)
    for j in range(4):
        expert = info[:, j:j + 1]
        mine = expert == lanes
        slot = jnp.sum(jnp.where(mine, rank, 0.0), axis=1, keepdims=True)
        here = wide == expert * float(CAP) + slot
        for p in range(3):
            coefs[p] = jnp.where(here, info[:, 4 + 4 * p + j:5 + 4 * p + j], coefs[p])
        line = dot(jnp.where(mine, 1.0, 0.0).astype(BF), table)
        value = jnp.sum(jnp.where(lanes == slot, line, 0.0), axis=1, keepdims=True)
        back = jnp.where(lanes == float(j), value, back)
    values = rows[...]
    total = dot(coefs[0].astype(BF), values) + (dot(coefs[1].astype(BF), values) + dot(coefs[2].astype(BF), values))
    out_ref[:, :WID] = total.astype(BF)
    out_ref[:, WID:] = back.astype(BF)


VM = pl.BlockSpec(memory_space=pltpu.VMEM)
SM = pl.BlockSpec(memory_space=pltpu.SMEM)


def call(kernel, out_shape, args, in_specs=None, scratch=(), name=None):
    return pl.pallas_call(
        kernel,
        out_shape=out_shape,
        in_specs=in_specs or [VM] * len(args),
        out_specs=jax.tree.map(lambda _: VM, out_shape),
        scratch_shapes=list(scratch),
        compiler_params=PARAMS,
        name=name,
    )(*args)


def struct(shape):
    return jax.ShapeDtypeStruct(shape, BF)


def shards(x_rollout, dest, route_ids, route_weights, cotangent, w_up, w_down):
    dp = lax.axis_size("dp")
    node = lax.axis_size("node")
    group = lax.axis_size("expert")
    me = lax.axis_index("dp")
    me_arr = me.reshape(1).astype(jnp.int32)
    swap = [(d * group + e, (e // 2) * group + 2 * d + e % 2) for d in range(dp) for e in range(group)]
    plane = ("node", "expert")

    sorted_x, pay = call(
        functools.partial(prepare_kernel, node * TOK),
        (struct((TOK, WID)), struct((TOK, WID + LANE))),
        (x_rollout, dest.reshape(1, TOK), cotangent, route_ids, route_weights),
        name="prepare",
    )
    pay = lax.ppermute(pay, ("dp", "expert"), swap)
    arrived = lax.all_to_all(sorted_x.reshape(dp, 32, WID), "dp", split_axis=0, concat_axis=0, tiled=True)
    moved_x = lax.ppermute(arrived.reshape(TOK, WID), ("dp", "expert"), swap)

    up, down = w_up[0], w_down[0]
    blocks = []
    for k in range(dp):
        start = lax.rem(me + k, dp) * 1024
        block = jnp.concatenate(
            [lax.dynamic_slice_in_dim(up, start, 1024, 1), lax.dynamic_slice_in_dim(down, start, 1024, 1)], axis=0
        )
        blocks.append(lax.ppermute(block, "dp", [(i, (i + k) % dp) for i in range(dp)]) if k else block)

    send = call(
        pack_kernel,
        struct((128, 48, LANE)),
        (pay, moved_x, jnp.asarray(np_pack(), BF)),
        scratch=(pltpu.VMEM((CAP, TOK, LANE), F32), pltpu.VMEM((TOK, 2 * WID), BF)),
        name="pack",
    )
    got = lax.all_to_all(send, plane, split_axis=0, concat_axis=0, tiled=True)
    part = call(
        forward_kernel,
        struct((4, 4, 96, WID)),
        (me_arr, got.reshape(node, group, 48, LANE), *blocks, jnp.asarray(np_unpack(), BF)),
        in_specs=[SM] + [VM] * 6,
        scratch=(pltpu.VMEM((384, 1024), BF), pltpu.VMEM((384, 1024), BF)),
        name="forward",
    )
    part = lax.all_to_all(part, "dp", split_axis=0, concat_axis=0, tiled=True)
    grad = call(act_kernel, struct((96, 1024 + LANE)), (part, jnp.asarray(np_slot_mask(), BF)), name="act")
    grads = lax.all_gather(grad, "dp", axis=0, tiled=False)
    reply = pl.pallas_call(
        backward_kernel,
        grid=(1,),
        out_shape=struct((node, group, 32, LANE)),
        in_specs=[SM, VM] + [pl.BlockSpec((256, 1024), lambda i: (0, 0))] * 4 + [VM],
        out_specs=VM,
        scratch_shapes=[pltpu.VMEM((384, 1024), BF)],
        compiler_params=PARAMS,
        name="backward",
    )(me_arr, grads, *blocks, jnp.asarray(np_reply(), BF))
    back = lax.all_to_all(reply.reshape(128, 32, LANE), plane, split_axis=0, concat_axis=0, tiled=True)
    result = call(
        combine_kernel,
        struct((TOK, WID + LANE)),
        (back, pay[:, WID:], jnp.asarray(np_collect(), BF)),
        scratch=(pltpu.VMEM((128 * CAP, WID), BF), pltpu.VMEM((LANE, LANE), F32)),
        name="combine",
    )
    result = lax.ppermute(result, ("dp", "expert"), swap)
    return result[:, :WID], result[:, WID:WID + 4]


def solution(mesh):
    in_specs = (
        P(("dp", "node"), "expert"),
        P(("dp", "node")),
        P(("dp", "node"), None),
        P(("dp", "node"), None),
        P(("dp", "node"), "expert"),
        P(("node", "expert"), "dp", None),
        P(("node", "expert"), "dp", None),
    )
    out_specs = (P(("dp", "node"), "expert"), P(("dp", "node"), None))
    return jax.shard_map(shards, mesh=mesh, in_specs=in_specs, out_specs=out_specs, check_vma=False)
```

time: 329 us -> 226 us (0.69)
  the two profiles are of different devices: /device:TPU:1 before, /device:TPU:15 now
where the time goes in v1:
time: 226 us; the launch traced here: 225 us
  waiting for transfers between devices  102 us (45%)
  starting transfers between devices  59.2 us (26%)
  blocking collectives  35.7 us (16%)
  local copies, waits for them, and re-layouts  15.6 us (7%)
  Pallas kernels  11 us (5%)
    ppermute x3, waiting for transfers between devices, shards(): lax.ppermute(block, 'dp', [(i, (i + k) % dp) for i in range(dp)])  39.9 us
    all_to_all x1, waiting for transfers between devices, shards(): lax.all_to_all(reply.reshape(128, 32, LANE), plane, split_axis=0, concat_...  30.3 us
    all_to_all x1, blocking collectives, shards(): part = lax.all_to_all(part, 'dp', split_axis=0, concat_axis=0, tiled=True)  23 us
    all_to_all x1, starting transfers between devices, shards(): lax.all_to_all(reply.reshape(128, 32, LANE), plane, split_axis=0, concat_...  16.5 us
    ppermute x1, waiting for transfers between devices, shards(): pay = lax.ppermute(pay, ('dp', 'expert'), swap)  15.2 us
    all_to_all x1, starting transfers between devices, shards(): got = lax.all_to_all(send, plane, split_axis=0, concat_axis=0, tiled=True)  15.2 us
    ppermute x1, waiting for transfers between devices, shards(): result = lax.ppermute(result, ('dp', 'expert'), swap)  13.9 us
    all_gather x1, blocking collectives, shards(): grads = lax.all_gather(grad, 'dp', axis=0, tiled=False)  12.7 us
  transfers between devices with their start and end apart: 9, of which 7 were waited for; matrix products, arithmetic and copies ran while one was open for 1% of the time, Pallas kernels for 0%

profile of v1, /device:TPU:15, one launch (start us, length us, event | category | flops | bytes accessed | tf_op | source)
XLA Modules:
  0.0 224.7 jit_solution(2526422829496686711)
XLA Ops:
  5.5 4.2 %all-to-all-start = ((bf16[4,32,512]{2,1,0:T(8,128)(2,1)}), bf16[4,32,512]{2,1,0:T(8,128)(2,1)S(1)}, u32[]{:S(2)}, u32[]{:S(2)}) async-start(bf16[4,32,512]{2,1,0:T(8,128)(2,1)} %bitcast.2), calls=%async_computation | async-start | bytes 262144 | tf_op jit(solution)/shard_map/all_to_all | solution.py:267
  9.7 4.7 %collective-permute-start = (bf16[128,640]{1,0:T(8,128)(2,1)S(1)}, bf16[128,640]{1,0:T(8,128)(2,1)S(1)}, u32[]{:S(2)}, u32[]{:S(2)}) collective-permute-start(bf16[128,640]{1,0:T(8,128)(2,1)S(1)} %get-tuple-element.4), channel_id=1, source_target_pairs={{0,0},{1,1},{2,128},{3,129},{4,256},{5,257},{6,384},{7,385},{128,2... | collective-permute-start | bytes 491528 | tf_op jit(solution)/shard_map/ppermute | solution.py:266
  14.4 4.8 %collective-permute-start.1 = (bf16[128,512]{1,0:T(8,128)(2,1)S(1)}, bf16[128,512]{1,0:T(8,128)(2,1)S(1)}, u32[]{:S(2)}, u32[]{:S(2)}) collective-permute-start(bf16[128,512]{1,0:T(8,128)(2,1)S(1)} %bitcast.26), channel_id=1, source_target_pairs={{0,0},{1,1},{2,128},{3,129},{4,256},{5,257},{6,384},{7,385},{128,2... | collective-permute-start | bytes 393224 | tf_op jit(solution)/shard_map/ppermute | solution.py:268
  19.3 15.2 %collective-permute-done.pay_ref = bf16[128,640]{1,0:T(8,128)(2,1)S(1)} collective-permute-done((bf16[128,640]{1,0:T(8,128)(2,1)S(1)}, bf16[128,640]{1,0:T(8,128)(2,1)S(1)}, u32[]{:S(2)}, u32[]{:S(2)}) %collective-permute-start) | collective-permute-done | bytes 163872 | tf_op jit(solution)/shard_map/ppermute | solution.py:266
  34.5 2.8 %collective-permute-done.1.x_ref = bf16[128,512]{1,0:T(8,128)(2,1)S(1)} collective-permute-done((bf16[128,512]{1,0:T(8,128)(2,1)S(1)}, bf16[128,512]{1,0:T(8,128)(2,1)S(1)}, u32[]{:S(2)}, u32[]{:S(2)}) %collective-permute-start.1) | collective-permute-done | bytes 131104 | tf_op jit(solution)/shard_map/ppermute | solution.py:268
  38.3 3.6 %pack.1 = bf16[128,48,128]{2,1,0:T(8,128)(2,1)} custom-call(bf16[128,640]{1,0:T(8,128)(2,1)S(1)} %collective-permute-done.pay_ref, bf16[128,512]{1,0:T(8,128)(2,1)S(1)} %collective-permute-done.1.x_ref, bf16[384,384]{1,0:T(8,128)(2,1)S(1)} %copy-done.10), custom_call_target="tpu_custom_call" | custom-call | tf_op jit(solution)/shard_map/pack/pallas_call | solution.py:236
  41.9 15.2 %all-to-all-start.1 = ((bf16[128,48,128]{2,1,0:T(8,128)(2,1)}), bf16[128,48,128]{2,1,0:T(8,128)(2,1)S(1)}, u32[]{:S(2)}, u32[]{:S(2)}) async-start(bf16[128,48,128]{2,1,0:T(8,128)(2,1)} %pack.1), calls=%async_computation.1 | async-start | bytes 3145728 | tf_op jit(solution)/shard_map/all_to_all | solution.py:286
  57.1 2.6 %dynamic-slice_bitcast_fusion = (bf16[256,1024]{1,0:T(8,128)(2,1)S(1)}, bf16[256,1024]{1,0:T(8,128)(2,1)S(1)}, bf16[256,1024]{1,0:T(8,128)(2,1)S(1)}, bf16[256,1...) fusion(bf16[1,256,4096]{2,1,0:T(8,128)(2,1)} %param.18, ...), kind=kLoop, calls=%fused_computation.4 | loop fusion | bytes 8388624 | tf_op jit(solution)/shard_map/dynamic_slice | solution.py:275
  59.8 3.5 %collective-permute-start.3 = (bf16[512,1024]{1,0:T(8,128)(2,1)S(1)}, bf16[512,1024]{1,0:T(8,128)(2,1)S(1)}, u32[]{:S(2)}, u32[]{:S(2)}) collective-permute-start(bf16[512,1024]{1,0:T(8,128)(2,1)S(1)} %pad_maximum_fusion.2), channel_id=1, source_target_pairs={{0,256},{128,384},{256,0},{384,128},{1,257},{129,385},{257,1},{385... | collective-permute-start | bytes 3145736 | tf_op jit(solution)/shard_map/ppermute | solution.py:277
  63.4 1.9 collective-permute-start.2
  65.4 3.4 %collective-permute-start.4 = (bf16[512,1024]{1,0:T(8,128)(2,1)S(1)}, bf16[512,1024]{1,0:T(8,128)(2,1)S(1)}, u32[]{:S(2)}, u32[]{:S(2)}) collective-permute-start(bf16[512,1024]{1,0:T(8,128)(2,1)S(1)} %pad_maximum_fusion.3), channel_id=1, source_target_pairs={{0,384},{128,0},{256,128},{384,256},{1,385},{129,1},{257,129},{385... | collective-permute-start | bytes 3145736 | tf_op jit(solution)/shard_map/ppermute | solution.py:277
  68.9 18.8 %collective-permute-done.3.w2 = bf16[512,1024]{1,0:T(8,128)(2,1)S(1)} collective-permute-done((bf16[512,1024]{1,0:T(8,128)(2,1)S(1)}, bf16[512,1024]{1,0:T(8,128)(2,1)S(1)}, u32[]{:S(2)}, u32[]{:S(2)}) %collective-permute-start.3) | collective-permute-done | bytes 1048608 | tf_op jit(solution)/shard_map/ppermute | solution.py:277
  88.6 20.0 %collective-permute-done.2.w1 = bf16[512,1024]{1,0:T(8,128)(2,1)S(1)} collective-permute-done((bf16[512,1024]{1,0:T(8,128)(2,1)S(1)}, bf16[512,1024]{1,0:T(8,128)(2,1)S(1)}, u32[]{:S(2)}, u32[]{:S(2)}) %collective-permute-start.2) | collective-permute-done | bytes 1048608 | tf_op jit(solution)/shard_map/ppermute | solution.py:277
  111.7 1.2 copy-done.1
  113.0 1.2 copy-done.4
  114.2 1.2 copy-done.7
  115.4 2.6 %forward.1 = bf16[4,4,96,512]{3,2,1,0:T(8,128)(2,1)S(1)} custom-call(s32[1]{0:T(128)} %bitcast.me_ref, bf16[16,8,48,128]{3,2,1,0:T(8,128)(2,1)S(1)} %bitcast.23, bf16[512,1024]{1,0:T(8,128)(2,1)S(1)} %pad_maximum_fusion.w0, bf16[512,1024]{1,0:T(8,128)(2,1)S(1)} %copy-done.4, bf16[512,1024]{1,0:T(8,128)(2,1)S(1)} %copy-done.1, ...), custom_call_target="tpu_custom_call" | custom-call | tf_op jit(solution)/shard_map/forward/pallas_call | solution.py:236
  118.0 23.0 %all_to_all.20.part_ref = bf16[4,4,96,512]{3,2,1,0:T(8,128)(2,1)S(1)} all-to-all(bf16[4,4,96,512]{3,2,1,0:T(8,128)(2,1)S(1)} %forward.1), channel_id=1, replica_groups=mesh['dp'=4,'node'=16,'expert'=8] {'dp'}, dimensions={0} | all-to-all | bytes 3145728 | tf_op jit(solution)/shard_map/all_to_all | solution.py:295
  141.4 12.7 %all-gather = bf16[384,1152]{1,0:T(8,128)(2,1)S(1)} all-gather(bf16[96,1152]{1,0:T(8,128)(2,1)S(1)} %act.1), channel_id=2, replica_groups=mesh['dp'=4,'node'=16,'expert'=8] {'dp'}, dimensions={0}, use_global_device_ids=true | all-gather | bytes 1105920 | tf_op jit(solution)/shard_map/all_gather | solution.py:297
  154.2 2.4 %backward.1 = bf16[16,8,32,128]{3,2,1,0:T(8,128)(2,1)} custom-call(s32[1]{0:T(128)} %bitcast.me_ref, bf16[4,96,1152]{2,1,0:T(8,128)(2,1)S(1)} %bitcast.24, bf16[512,1024]{1,0:T(8,128)(2,1)S(1)} %pad_maximum_fusion.w0, bf16[512,1024]{1,0:T(8,128)(2,1)S(1)} %copy-done.5, bf16[512,1024]{1,0:T(8,128)(2,1)S(1)} %copy-done.2, bf16[512,1024]{1,0:T(8,128)(2,1)S(1)} %copy-done.8, ...), custom_call_target="tpu_custom_call" | custom-call | tf_op jit(solution)/shard_map/backward/pallas_call | solution.py:298
  156.5 16.5 %all-to-all-start.3 = ((bf16[128,32,128]{2,1,0:T(8,128)(2,1)}), bf16[128,32,128]{2,1,0:T(8,128)(2,1)S(1)}, u32[]{:S(2)}, u32[]{:S(2)}) async-start(bf16[128,32,128]{2,1,0:T(8,128)(2,1)} %bitcast.14), calls=%async_computation.3 | async-start | bytes 2097152 | tf_op jit(solution)/shard_map/all_to_all | solution.py:308
  173.1 30.3 %all-to-all-done.3.got_ref = bf16[128,32,128]{2,1,0:T(8,128)(2,1)S(1)} async-done(((bf16[128,32,128]{2,1,0:T(8,128)(2,1)}), bf16[128,32,128]{2,1,0:T(8,128)(2,1)S(1)}, u32[]{:S(2)}, u32[]{:S(2)}) %all-to-all-start.3) | async-done | bytes 1048608 | tf_op jit(solution)/shard_map/all_to_all | solution.py:308
  204.5 5.0 %collective-permute-start.5 = (bf16[128,640]{1,0:T(8,128)(2,1)S(1)}, bf16[128,640]{1,0:T(8,128)(2,1)S(1)}, u32[]{:S(2)}, u32[]{:S(2)}) collective-permute-start(bf16[128,640]{1,0:T(8,128)(2,1)S(1)} %combine.1), channel_id=1, source_target_pairs={{0,0},{1,1},{2,128},{3,129},{4,256},{5,257},{6,384},{7,385},{128,2... | collective-permute-start | bytes 491528 | tf_op jit(solution)/shard_map/ppermute | solution.py:316
  209.5 13.9 %collective-permute-done.5 = bf16[128,640]{1,0:T(8,128)(2,1)S(1)} collective-permute-done((bf16[128,640]{1,0:T(8,128)(2,1)S(1)}, bf16[128,640]{1,0:T(8,128)(2,1)S(1)}, u32[]{:S(2)}, u32[]{:S(2)}) %collective-permute-start.5) | collective-permute-done | bytes 163872 | tf_op jit(solution)/shard_map/ppermute | solution.py:316
  (47 shorter events, 13.2 us)
Async XLA Ops:
  2.2 0.9 copy-start.12
  5.5 8.9 %all-to-all-start = ((bf16[4,32,512]{2,1,0:T(8,128)(2,1)}), bf16[4,32,512]{2,1,0:T(8,128)(2,1)S(1)}, u32[]{:S(2)}, u32[]{:S(2)}) async-start(bf16[4,32,512]{2,1,0:T(8,128)(2,1)} %bitcast.2), calls=%async_computation | async-start | bytes 262144 | tf_op jit(solution)/shard_map/all_to_all | solution.py:267
  9.7 24.7 %collective-permute-start = (bf16[128,640]{1,0:T(8,128)(2,1)S(1)}, bf16[128,640]{1,0:T(8,128)(2,1)S(1)}, u32[]{:S(2)}, u32[]{:S(2)}) collective-permute-start(bf16[128,640]{1,0:T(8,128)(2,1)S(1)} %get-tuple-element.4), channel_id=1, source_target_pairs={{0,0},{1,1},{2,128},{3,129},{4,256},{5,257},{6,384},{7,385},{128,2... | collective-permute-start | bytes 491528 | tf_op jit(solution)/shard_map/ppermute | solution.py:266
  14.4 22.8 %collective-permute-start.1 = (bf16[128,512]{1,0:T(8,128)(2,1)S(1)}, bf16[128,512]{1,0:T(8,128)(2,1)S(1)}, u32[]{:S(2)}, u32[]{:S(2)}) collective-permute-start(bf16[128,512]{1,0:T(8,128)(2,1)S(1)} %bitcast.26), channel_id=1, source_target_pairs={{0,0},{1,1},{2,128},{3,129},{4,256},{5,257},{6,384},{7,385},{128,2... | collective-permute-start | bytes 393224 | tf_op jit(solution)/shard_map/ppermute | solution.py:268
  37.3 1.0 copy-start.10
  41.9 69.9 %all-to-all-start.1 = ((bf16[128,48,128]{2,1,0:T(8,128)(2,1)}), bf16[128,48,128]{2,1,0:T(8,128)(2,1)S(1)}, u32[]{:S(2)}, u32[]{:S(2)}) async-start(bf16[128,48,128]{2,1,0:T(8,128)(2,1)} %pack.1), calls=%async_computation.1 | async-start | bytes 3145728 | tf_op jit(solution)/shard_map/all_to_all | solution.py:286
  59.8 27.8 %collective-permute-start.3 = (bf16[512,1024]{1,0:T(8,128)(2,1)S(1)}, bf16[512,1024]{1,0:T(8,128)(2,1)S(1)}, u32[]{:S(2)}, u32[]{:S(2)}) collective-permute-start(bf16[512,1024]{1,0:T(8,128)(2,1)S(1)} %pad_maximum_fusion.2), channel_id=1, source_target_pairs={{0,256},{128,384},{256,0},{384,128},{1,257},{129,385},{257,1},{385... | collective-permute-start | bytes 3145736 | tf_op jit(solution)/shard_map/ppermute | solution.py:277
  63.4 45.2 %collective-permute-start.2 = (bf16[512,1024]{1,0:T(8,128)(2,1)S(1)}, bf16[512,1024]{1,0:T(8,128)(2,1)S(1)}, u32[]{:S(2)}, u32[]{:S(2)}) collective-permute-start(bf16[512,1024]{1,0:T(8,128)(2,1)S(1)} %pad_maximum_fusion.1), channel_id=1, source_target_pairs={{0,128},{128,256},{256,384},{384,0},{1,129},{129,257},{257,385},{3... | collective-permute-start | bytes 3145736 | tf_op jit(solution)/shard_map/ppermute | solution.py:277
  65.3 46.4 %copy-start.9 = (bf16[384,384]{1,0:T(8,128)(2,1)S(1)}, bf16[384,384]{1,0:T(8,128)(2,1)}, u32[]{:S(2)}) copy-start(bf16[384,384]{1,0:T(8,128)(2,1)} %constant.46.clone.perm_ref) | copy-start | bytes 884740
  65.4 45.3 %collective-permute-start.4 = (bf16[512,1024]{1,0:T(8,128)(2,1)S(1)}, bf16[512,1024]{1,0:T(8,128)(2,1)S(1)}, u32[]{:S(2)}, u32[]{:S(2)}) collective-permute-start(bf16[512,1024]{1,0:T(8,128)(2,1)S(1)} %pad_maximum_fusion.3), channel_id=1, source_target_pairs={{0,384},{128,0},{256,128},{384,256},{1,385},{129,1},{257,129},{385... | collective-permute-start | bytes 3145736 | tf_op jit(solution)/shard_map/ppermute | solution.py:277
  87.6 1.0 copy-start
  108.5 1.0 copy-start.3
  110.7 1.0 copy-start.6
  111.7 1.2 copy-start.1
  113.0 1.2 copy-start.4
  114.2 1.2 copy-start.7
  118.0 23.0 %copy-start.15 = (bf16[96,128]{1,0:T(8,128)(2,1)S(1)}, bf16[96,128]{1,0:T(8,128)(2,1)}, u32[]{:S(2)}) copy-start(bf16[96,128]{1,0:T(8,128)(2,1)} %constant.47.clone.mask_ref) | copy-start | bytes 73732
  118.0 36.1 %copy-start.8 = (bf16[512,1024]{1,0:T(8,128)(2,1)S(1)}, bf16[512,1024]{1,0:T(8,128)(2,1)}, u32[]{:S(2)}) copy-start(bf16[512,1024]{1,0:T(8,128)(2,1)} %copy-done.6) | copy-start | bytes 3145732
  141.0 13.1 %copy-start.2 = (bf16[512,1024]{1,0:T(8,128)(2,1)S(1)}, bf16[512,1024]{1,0:T(8,128)(2,1)}, u32[]{:S(2)}) copy-start(bf16[512,1024]{1,0:T(8,128)(2,1)} %copy-done) | copy-start | bytes 3145732
  141.1 13.1 %copy-start.5 = (bf16[512,1024]{1,0:T(8,128)(2,1)S(1)}, bf16[512,1024]{1,0:T(8,128)(2,1)}, u32[]{:S(2)}) copy-start(bf16[512,1024]{1,0:T(8,128)(2,1)} %copy-done.3) | copy-start | bytes 3145732
  141.1 13.1 %copy-start.11 = (bf16[256,256]{1,0:T(8,128)(2,1)S(1)}, bf16[256,256]{1,0:T(8,128)(2,1)}, u32[]{:S(2)}) copy-start(bf16[256,256]{1,0:T(8,128)(2,1)} %constant.48.clone.perm_ref) | copy-start | bytes 393220
  156.5 46.8 %copy-start.14 = (bf16[208,256]{1,0:T(8,128)(2,1)S(1)}, bf16[208,256]{1,0:T(8,128)(2,1)}, u32[]{:S(2)}) copy-start(bf16[208,256]{1,0:T(8,128)(2,1)} %constant.49.clone.perm_ref) | copy-start | bytes 319492
  156.5 46.8 %all-to-all-start.3 = ((bf16[128,32,128]{2,1,0:T(8,128)(2,1)}), bf16[128,32,128]{2,1,0:T(8,128)(2,1)S(1)}, u32[]{:S(2)}, u32[]{:S(2)}) async-start(bf16[128,32,128]{2,1,0:T(8,128)(2,1)} %bitcast.14), calls=%async_computation.3 | async-start | bytes 2097152 | tf_op jit(solution)/shard_map/all_to_all | solution.py:308
  204.5 18.9 %collective-permute-start.5 = (bf16[128,640]{1,0:T(8,128)(2,1)S(1)}, bf16[128,640]{1,0:T(8,128)(2,1)S(1)}, u32[]{:S(2)}, u32[]{:S(2)}) collective-permute-start(bf16[128,640]{1,0:T(8,128)(2,1)S(1)} %combine.1), channel_id=1, source_target_pairs={{0,0},{1,1},{2,128},{3,129},{4,256},{5,257},{6,384},{7,385},{128,2... | collective-permute-start | bytes 491528 | tf_op jit(solution)/shard_map/ppermute | solution.py:316
  (2 other events, 1.6 us)

commit v2 on v1

v2 whole, which is shorter than its diff:
```python
import functools

import jax
import jax.numpy as jnp
from jax import lax
from jax.experimental import pallas as pl
from jax.experimental.pallas import tpu as pltpu
from jax.sharding import PartitionSpec as P

BF = jnp.bfloat16
F32 = jnp.float32
CAP = 6
TOK = 128
WID = 512
INFO = 16
LANE = 128
GATHER_BYTES = 200_000_000
PARAMS = pltpu.CompilerParams(vmem_limit_bytes=20 * 1024 * 1024)


def iota(shape, dim):
    return lax.broadcasted_iota(jnp.int32, shape, dim)


def split(index, base):
    high = jnp.floor((index + 0.5) * (1.0 / base))
    return high, index - high * base


def order_matrix(rows, columns, source):
    row = iota((rows, 1), 0).astype(F32)
    return jnp.where(iota((rows, columns), 1).astype(F32) == source(row), 1.0, 0.0).astype(BF)


def pack_source(row):
    expert, rest = split(row, 48)
    chunk, slot = split(rest, CAP)
    return chunk * 48 + slot * 8 + expert


def unpack_source(row):
    chunk, rest = split(row, 48)
    node, slot = split(rest, CAP)
    return node * 48 + chunk * CAP + slot


def collect_source(row):
    chunk, rest = split(row, 48)
    expert, slot = split(rest, CAP)
    return jnp.where(row < 192, expert * 32 + chunk * CAP + slot, jnp.where(row < 200, (row - 192) * 32 + 24, -1.0))


def reply_matrix():
    column = iota((1, 256), 1).astype(F32)
    chunk, rest = split(column, 48)
    node, slot = split(rest, CAP)
    target = jnp.where(column < 192, node * 32 + chunk * CAP + slot, jnp.where(column < 240, node * 32 + 24, -1.0))
    return jnp.where(iota((256, 256), 0).astype(F32) == target, 1.0, 0.0).astype(BF)


def dot(a, b):
    return jnp.dot(a, b, preferred_element_type=F32)


def dot_nt(a, b):
    return lax.dot_general(a, b, (((1,), (1,)), ((), ())), preferred_element_type=F32)


def dot_tn(a, b):
    return lax.dot_general(a, b, (((0,), (0,)), ((), ())), preferred_element_type=F32)


def named_rows(info):
    experts = iota((LANE, TOK), 0).astype(F32)
    named = jnp.zeros((LANE, TOK), F32)
    for j in range(4):
        named = named + jnp.where(info[j:j + 1, :] == experts, 1.0, 0.0)
    earlier = jnp.where(iota((TOK, TOK), 0) < iota((TOK, TOK), 1), 1.0, 0.0).astype(BF)
    return named, dot(named.astype(BF), earlier)


def prepare_kernel(shard_step, x_any, dest_any, dy_any, ids_any, w_any, sorted_ref, pay_ref,
                   x_ref, dest_ref, ids_ref, w_ref, sems):
    copies = [
        pltpu.make_async_copy(source, target, sems.at[i])
        for i, (source, target) in enumerate((
            (dest_any, dest_ref), (ids_any, ids_ref), (w_any, w_ref), (x_any, x_ref), (dy_any, pay_ref.at[:TOK]),
        ))
    ]
    for copy in copies:
        copy.start()
    pay_ref[TOK:, LANE:] = jnp.zeros((INFO, WID - LANE), BF)
    for copy in copies:
        copy.wait()
    dest = dest_ref[...]
    target = (dest // shard_step) * 32 + (dest % TOK) // 4
    pick = jnp.where(iota((TOK, TOK), 0) == target, 1.0, 0.0).astype(BF)
    sorted_ref[...] = dot(pick, x_ref[...]).astype(BF)
    weights = w_ref[...]
    high = weights.astype(BF).astype(F32)
    middle = (weights - high).astype(BF).astype(F32)
    low = weights - high - middle
    pay_ref[TOK:, :LANE] = jnp.concatenate([ids_ref[...].astype(F32), high, middle, low], axis=0).astype(BF)


def split_kernel(me_ref, up_ref, down_ref, after_ref, *refs):
    outs, sems = refs[:4], refs[4]
    copies = []
    for k in range(4):
        start = pl.multiple_of(lax.rem(me_ref[0] + k, 4) * 1024, 1024)
        for h, w in enumerate((up_ref, down_ref)):
            copies.append(pltpu.make_async_copy(
                w.at[:, pl.ds(start, 1024)], outs[k].at[h * 256:h * 256 + 256], sems.at[2 * k + h]
            ))
    for copy in copies:
        copy.start()
    for copy in copies:
        copy.wait()


def pack_kernel(pay_ref, x_ref, out_ref, slots, rows):
    named, rank = named_rows(pay_ref[TOK:, :LANE].astype(F32))
    for s in range(CAP):
        slots[s] = jnp.where(rank == float(s), named, 0.0)
    token = iota((TOK, TOK), 0)
    order = jnp.where(iota((TOK, TOK), 1) == (token % 4) * 32 + token // 4, 1.0, 0.0).astype(BF)
    rows[:, :WID] = pay_ref[:TOK, :]
    rows[:, WID:] = dot(order, x_ref[...]).astype(BF)
    perm = order_matrix(384, 384, pack_source)
    for pair in range(8):
        halves = []
        for block in (2 * pair, 2 * pair + 1):
            pick = jnp.concatenate([slots[s, block * 8:block * 8 + 8, :] for s in range(CAP)], axis=0).astype(BF)
            got = dot(pick, rows[...]).astype(BF)
            halves.append(jnp.concatenate([got[:, a * LANE:(a + 1) * LANE] for a in range(8)], axis=0))
        sent = dot(perm, jnp.concatenate(halves, axis=1)).astype(BF)
        for h in range(2):
            out_ref[(2 * pair + h) * 8:(2 * pair + h) * 8 + 8] = sent[:, h * LANE:(h + 1) * LANE].reshape(8, 48, LANE)


def gather_kernel(me_ref, w0, w1, w2, w3, out_ref):
    me = me_ref[0]
    for k, w in enumerate((w0, w1, w2, w3)):
        block = lax.rem(me - k + 4, 4)
        out_ref[0, block] = w[:256]
        out_ref[1, block] = w[256:]


def forward_kernel(me_ref, got_ref, w_ref, out_ref, dy_rows, x_rows):
    perm = order_matrix(384, 384, unpack_source)
    me = me_ref[0]
    for d in range(4):
        place = 2 * jnp.bitwise_xor(me, d)
        for half in range(2):
            base = d * 96 + half * 48
            both = jnp.concatenate(
                [got_ref[half * 8:half * 8 + 8, place + b].reshape(384, LANE) for b in range(2)], axis=1
            )
            moved = dot(perm, both).astype(BF)
            for a in range(8):
                target = dy_rows if a < 4 else x_rows
                for b in range(2):
                    col = (b * 4 + a % 4) * LANE
                    target[base:base + 48, col:col + LANE] = moved[a * 48:a * 48 + 48, b * LANE:(b + 1) * LANE]
    for block in range(4):
        pre = dot_nt(x_rows[...], w_ref[0, block]).astype(BF)
        grad = dot_nt(dy_rows[...], w_ref[1, block]).astype(BF)
        out_ref[:, block, :, :256] = pre.reshape(4, 96, 256)
        out_ref[:, block, :, 256:] = grad.reshape(4, 96, 256)


def act_kernel(part_ref, out_ref):
    score = jnp.zeros((96, 1), F32)
    for block in range(4):
        total = part_ref[0, block].astype(F32)
        for s in range(1, 4):
            total = total + part_ref[s, block].astype(F32)
        pre = total[:, :256]
        grad = total[:, 256:]
        sig = jax.nn.sigmoid(pre)
        score = score + jnp.sum(pre * sig * grad, axis=1, keepdims=True)
        out_ref[:, block * 256:block * 256 + 256] = (grad * sig * (1.0 + pre * (1.0 - sig))).astype(BF)
    _, slot = split(iota((96, 1), 0).astype(F32), CAP)
    out_ref[:, 1024:] = jnp.where(iota((96, LANE), 1).astype(F32) == slot, score, 0.0).astype(BF)


def backward_kernel(me_ref, grad_ref, w_ref, out_ref, rows):
    total = jnp.zeros((384, 1024), F32)
    for block in range(4):
        part = grad_ref[:, :, block * 256:block * 256 + 256].reshape(384, 256)
        total = total + dot(part, w_ref[0, block])
    rows[...] = total.astype(BF)
    perm = reply_matrix()
    me = me_ref[0]
    for d in range(4):
        place = 2 * jnp.bitwise_xor(me, d)
        for half in range(2):
            base = d * 96 + half * 48
            score = grad_ref[d, half * 48:half * 48 + 48, 1024:]
            stacks = []
            for b in range(2):
                parts = [rows[base:base + 48, (b * 4 + c) * LANE:(b * 4 + c + 1) * LANE] for c in range(4)]
                stacks.append(jnp.concatenate(parts + [score, jnp.zeros((16, LANE), BF)], axis=0))
            sent = dot(perm, jnp.concatenate(stacks, axis=1)).astype(BF)
            for b in range(2):
                out_ref[half * 8:half * 8 + 8, place + b] = sent[:, b * LANE:(b + 1) * LANE].reshape(8, 32, LANE)


def combine_kernel(got_ref, pay_ref, out_ref, rows, scores):
    info_rows = pay_ref[TOK:, :LANE]
    named, rank_rows = named_rows(info_rows.astype(F32))
    eye = jnp.where(iota((TOK, TOK), 0) == iota((TOK, TOK), 1), 1.0, 0.0).astype(BF)
    rank = dot_tn(rank_rows.astype(BF), eye)
    info = dot_tn(info_rows, eye[:INFO])
    perm = order_matrix(208, 256, collect_source)
    for pair in range(8):
        both = jnp.concatenate(
            [got_ref[(2 * pair + h) * 8:(2 * pair + h) * 8 + 8].reshape(256, LANE) for h in range(2)], axis=1
        )
        moved = dot(perm, both)
        for h in range(2):
            block = 2 * pair + h
            half = moved[:, h * LANE:(h + 1) * LANE]
            scores[block * 8:block * 8 + 8] = half[192:200]
            for c in range(4):
                rows[block * 48:block * 48 + 48, c * LANE:(c + 1) * LANE] = half[c * 48:c * 48 + 48].astype(BF)
    lanes = iota((TOK, LANE), 1).astype(F32)
    wide = iota((TOK, 128 * CAP), 1).astype(F32)
    coefs = [jnp.zeros((TOK, 128 * CAP), F32) for _ in range(3)]
    table = scores[...].astype(BF)
    back = jnp.zeros((TOK, LANE), F32)
    for j in range(4):
        expert = info[:, j:j + 1]
        mine = expert == lanes
        slot = jnp.sum(jnp.where(mine, rank, 0.0), axis=1, keepdims=True)
        here = wide == expert * float(CAP) + slot
        for p in range(3):
            coefs[p] = jnp.where(here, info[:, 4 + 4 * p + j:5 + 4 * p + j], coefs[p])
        line = dot(jnp.where(mine, 1.0, 0.0).astype(BF), table)
        value = jnp.sum(jnp.where(lanes == slot, line, 0.0), axis=1, keepdims=True)
        back = jnp.where(lanes == float(j), value, back)
    values = rows[...]
    total = dot(coefs[0].astype(BF), values) + (dot(coefs[1].astype(BF), values) + dot(coefs[2].astype(BF), values))
    out_ref[:TOK, :] = total.astype(BF)
    out_ref[TOK:, :LANE] = dot_tn(back.astype(BF), eye)[:INFO].astype(BF)
    out_ref[TOK:, LANE:] = jnp.zeros((INFO, WID - LANE), BF)


VM = pl.BlockSpec(memory_space=pltpu.VMEM)
SM = pl.BlockSpec(memory_space=pltpu.SMEM)
HBM = pl.BlockSpec(memory_space=pltpu.HBM)


def call(kernel, out_shape, args, in_specs=None, scratch=(), name=None, cost=None, out_spec=VM, params=PARAMS):
    return pl.pallas_call(
        kernel,
        out_shape=out_shape,
        in_specs=in_specs or [VM] * len(args),
        out_specs=jax.tree.map(lambda _: out_spec, out_shape),
        scratch_shapes=list(scratch),
        compiler_params=params,
        cost_estimate=cost,
        name=name,
    )(*args)


def struct(shape):
    return jax.ShapeDtypeStruct(shape, BF)


def shards(x_rollout, dest, route_ids, route_weights, cotangent, w_up, w_down):
    dp = lax.axis_size("dp")
    node = lax.axis_size("node")
    group = lax.axis_size("expert")
    me = lax.axis_index("dp")
    me_arr = me.reshape(1).astype(jnp.int32)
    swap = [(d * group + e, (e // 2) * group + 2 * (d ^ (e // 2)) + e % 2) for d in range(dp) for e in range(group)]
    swap_back = [(to, source) for source, to in swap]
    plane = ("node", "expert")

    sorted_x, pay = call(
        functools.partial(prepare_kernel, node * TOK),
        (struct((TOK, WID)), struct((TOK + INFO, WID))),
        (x_rollout, dest.reshape(1, TOK), cotangent, route_ids.T, route_weights.T),
        in_specs=[HBM] * 5,
        scratch=(
            pltpu.VMEM((TOK, WID), BF), pltpu.VMEM((1, TOK), jnp.int32), pltpu.VMEM((4, TOK), jnp.int32),
            pltpu.VMEM((4, TOK), F32), pltpu.SemaphoreType.DMA((5,)),
        ),
        params=pltpu.CompilerParams(vmem_limit_bytes=48 * 1024 * 1024),
        name="prepare",
    )
    pay = lax.ppermute(pay, ("dp", "expert"), swap)
    arrived = lax.all_to_all(sorted_x.reshape(dp, 32, WID), "dp", split_axis=0, concat_axis=0, tiled=True)
    moved_x = lax.ppermute(arrived.reshape(TOK, WID), ("dp", "expert"), swap)

    blocks = call(
        split_kernel,
        [struct((512, 1024))] * 4,
        (me_arr, w_up[0], w_down[0], arrived),
        in_specs=[SM, HBM, HBM, pl.BlockSpec(memory_space=pl.ANY)],
        out_spec=HBM,
        scratch=(pltpu.SemaphoreType.DMA((8,)),),
        name="split",
    )
    pay, moved_x, blocks = lax.optimization_barrier((pay, moved_x, blocks))
    blocks = [
        lax.ppermute(block, "dp", [(i, (i + k) % dp) for i in range(dp)]) if k else block
        for k, block in enumerate(blocks)
    ]
    send = call(
        pack_kernel,
        struct((128, 48, LANE)),
        (pay, moved_x),
        scratch=(pltpu.VMEM((CAP, TOK, LANE), F32), pltpu.VMEM((TOK, 2 * WID), BF)),
        name="pack",
    )
    got = lax.cond(
        me >= 0,
        lambda v: lax.all_to_all(v, plane, split_axis=0, concat_axis=0, tiled=True),
        lambda v: v,
        send,
    )
    got, blocks = lax.optimization_barrier((got, blocks))
    weights = call(
        gather_kernel,
        struct((2, 4, 256, 1024)),
        (me_arr, *blocks),
        in_specs=[SM] + [VM] * 4,
        name="gather",
        cost=pl.CostEstimate(flops=0, bytes_accessed=GATHER_BYTES, transcendentals=0),
    )
    part = call(
        forward_kernel,
        struct((4, 4, 96, WID)),
        (me_arr, got.reshape(node, group, 48, LANE), weights),
        in_specs=[SM, VM, VM],
        scratch=(pltpu.VMEM((384, 1024), BF), pltpu.VMEM((384, 1024), BF)),
        name="forward",
    )
    part = lax.all_to_all(part, "dp", split_axis=0, concat_axis=0, tiled=True)
    grad = call(act_kernel, struct((96, 1024 + LANE)), (part,), name="act")
    grads = lax.all_gather(grad, "dp", axis=0, tiled=False)
    reply = call(
        backward_kernel,
        struct((node, group, 32, LANE)),
        (me_arr, grads, weights),
        in_specs=[SM, VM, VM],
        scratch=(pltpu.VMEM((384, 1024), BF),),
        name="backward",
    )
    back = lax.all_to_all(reply.reshape(128, 32, LANE), plane, split_axis=0, concat_axis=0, tiled=True)
    result = call(
        combine_kernel,
        struct((TOK + INFO, WID)),
        (back, pay),
        scratch=(pltpu.VMEM((128 * CAP, WID), BF), pltpu.VMEM((LANE, LANE), F32)),
        name="combine",
    )
    result = lax.ppermute(result, ("dp", "expert"), swap_back)
    return result[:TOK], result[TOK:TOK + 4, :LANE].T


def solution(mesh):
    in_specs = (
        P(("dp", "node"), "expert"),
        P(("dp", "node")),
        P(("dp", "node"), None),
        P(("dp", "node"), None),
        P(("dp", "node"), "expert"),
        P(("node", "expert"), "dp", None),
        P(("node", "expert"), "dp", None),
    )
    out_specs = (P(("dp", "node"), "expert"), P(("dp", "node"), None))
    return jax.shard_map(shards, mesh=mesh, in_specs=in_specs, out_specs=out_specs, check_vma=False)
```

time: 226 us -> 207 us (0.916)
  blocking collectives: 35.7 us -> 139 us
  waiting for transfers between devices: 102 us -> 16.5 us
  starting transfers between devices: 59.2 us -> 26.5 us
  local copies, waits for them, and re-layouts: 15.6 us -> 9.71 us
  Pallas kernels: 11 us -> 13.7 us
    all_to_all x0 -> x2, blocking collectives: none -> 102 us  [the longest x1 62.7 us: shards(): lax.all_to_all(v, plane, split_axis=0, concat_axis=0, tiled=True)]
    ppermute x3, waiting for transfers between devices: 39.9 us -> 0.01 us  [shards(): lax.ppermute(block, 'dp', [(i, (i + k) % dp) for i in range(dp)])]
    all_to_all x2 -> x0, starting transfers between devices: 31.7 us -> none  [the longest x1 16.5 us: shards(): lax.all_to_all(reply.reshape(128, 32, LANE), plane, split_axis=0, concat_...]
    all_to_all x2 -> x0, waiting for transfers between devices: 30.3 us -> none  [the longest x1 30.3 us: shards(): lax.all_to_all(reply.reshape(128, 32, LANE), plane, split_axis=0, concat_...]
    ppermute x1, waiting for transfers between devices: 15.2 us -> 0.01 us  [shards(): pay = lax.ppermute(pay, ('dp', 'expert'), swap)]
    unnamed x37 -> x16, local copies, waits for them, and re-layouts: 12.3 us -> 7.08 us
    pallas_call x5 -> x8, Pallas kernels: 8.64 us -> 13.7 us  [call(): pl.pallas_call(kernel, out_shape=out_shape, in_specs=in_specs or [VM] * l...]
    dynamic_slice x1 -> x0, local copies, waits for them, and re-layouts: 2.62 us -> none  [shards(): lax.dynamic_slice_in_dim(down, start, 1024, 1)]
  transfers between devices with their start and end apart: 9 -> 7, of which waited for: 7 -> 2; matrix products, arithmetic and copies ran while one was open for 1% -> 0% of each run, Pallas kernels for 0% -> 3%
where the time goes in v2:
time: 207 us; the launch traced here: 206 us
  blocking collectives  139 us (67%)
  starting transfers between devices  26.5 us (13%)
  waiting for transfers between devices  16.5 us (8%)
  Pallas kernels  13.7 us (7%)
  local copies, waits for them, and re-layouts  9.71 us (5%)
    all_to_all x1, blocking collectives, shards(): lax.all_to_all(v, plane, split_axis=0, concat_axis=0, tiled=True)  62.7 us
    all_to_all x1, blocking collectives, shards(): lax.all_to_all(reply.reshape(128, 32, LANE), plane, split_axis=0, concat_...  39.6 us
    all_to_all x1, blocking collectives, shards(): part = lax.all_to_all(part, 'dp', split_axis=0, concat_axis=0, tiled=True)  24.5 us
    ppermute x1, waiting for transfers between devices, shards(): result = lax.ppermute(result, ('dp', 'expert'), swap_back)  14.7 us
    pallas_call x8, Pallas kernels, call(): pl.pallas_call(kernel, out_shape=out_shape, in_specs=in_specs or [VM] * l...  13.7 us
    all_gather x1, blocking collectives, shards(): grads = lax.all_gather(grad, 'dp', axis=0, tiled=False)  12.4 us
    ppermute x3, starting transfers between devices, shards(): lax.ppermute(block, 'dp', [(i, (i + k) % dp) for i in range(dp)])  9.72 us
    unnamed x16, local copies, waits for them, and re-layouts  7.08 us
  transfers between devices with their start and end apart: 7, of which 2 were waited for; matrix products, arithmetic and copies ran while one was open for 0% of the time, Pallas kernels for 3%

profile of v2, /device:TPU:15, one launch (start us, length us, event | category | flops | bytes accessed | tf_op | source)
XLA Modules:
  0.0 206.4 jit_solution(11997675512432947536)
XLA Ops:
  4.5 1.2 prepare.1
  5.7 4.2 %all-to-all-start.1 = ((bf16[4,32,512]{2,1,0:T(8,128)(2,1)}), bf16[4,32,512]{2,1,0:T(8,128)(2,1)S(1)}, u32[]{:S(2)}, u32[]{:S(2)}) async-start(bf16[4,32,512]{2,1,0:T(8,128)(2,1)} %bitcast.4), calls=%async_computation.1 | async-start | bytes 262144 | tf_op jit(solution)/shard_map/all_to_all | solution.py:294
  9.9 4.7 %collective-permute-start = (bf16[144,512]{1,0:T(8,128)(2,1)S(1)}, bf16[144,512]{1,0:T(8,128)(2,1)S(1)}, u32[]{:S(2)}, u32[]{:S(2)}) collective-permute-start(bf16[144,512]{1,0:T(8,128)(2,1)S(1)} %get-tuple-element.24), channel_id=1, source_target_pairs={{0,0},{1,1},{2,130},{3,131},{4,260},{5,261},{6,390},{7,391},{128,2... | collective-permute-start | bytes 442376 | tf_op jit(solution)/shard_map/ppermute | solution.py:293
  14.6 4.8 %collective-permute-start.1 = (bf16[128,512]{1,0:T(8,128)(2,1)S(1)}, bf16[128,512]{1,0:T(8,128)(2,1)S(1)}, u32[]{:S(2)}, u32[]{:S(2)}) collective-permute-start(bf16[128,512]{1,0:T(8,128)(2,1)S(1)} %bitcast.17), channel_id=1, source_target_pairs={{0,0},{1,1},{2,130},{3,131},{4,260},{5,261},{6,390},{7,391},{128,2... | collective-permute-start | bytes 393224 | tf_op jit(solution)/shard_map/ppermute | solution.py:295
  19.4 1.6 copy-done
  21.0 1.6 copy-done.1
  22.6 1.8 split.1
  24.4 1.7 collective-permute-done.1.x_ref
  26.2 1.9 collective-permute-start.2
  28.1 5.9 %collective-permute-start.3 = (bf16[512,1024]{1,0:T(8,128)(2,1)}, bf16[512,1024]{1,0:T(8,128)(2,1)S(1)}, u32[]{:S(2)}, u32[]{:S(2)}) collective-permute-start(bf16[512,1024]{1,0:T(8,128)(2,1)} %get-tuple-element.34), channel_id=1, source_target_pairs={{0,256},{128,384},{256,0},{384,128},{1,257},{129,385},{257,1},{385... | collective-permute-start | bytes 3145736 | tf_op jit(solution)/shard_map/ppermute | solution.py:308
  34.0 1.9 collective-permute-start.4
  35.9 3.4 %pack.1 = bf16[128,48,128]{2,1,0:T(8,128)(2,1)} custom-call(bf16[144,512]{1,0:T(8,128)(2,1)S(1)} %collective-permute-done.pay_ref, bf16[128,512]{1,0:T(8,128)(2,1)S(1)} %collective-permute-done.1.x_ref), custom_call_target="tpu_custom_call" | custom-call | tf_op jit(solution)/shard_map/pack/pallas_call | solution.py:255
  39.4 64.1 %conditional.1 = (bf16[128,48,128]{2,1,0:T(8,128)(2,1)}) conditional(s32[]{:T(128)} %convert_element_type.3, bf16[128,48,128]{2,1,0:T(8,128)(2,1)} %pack.1, bf16[128,48,128]{2,1,0:T(8,128)(2,1)} %pack.1), branch_computations={%region_0.0_spmd, %region_1.0_spmd} | conditional | bytes 9437220 | solution.py:318
  39.4 1.4 copy-done.8
  40.8 62.7 %all_to_all.19 = bf16[128,48,128]{2,1,0:T(8,128)(2,1)} all-to-all(bf16[128,48,128]{2,1,0:T(8,128)(2,1)S(1)} %copy-done.8), channel_id=1, replica_groups=mesh['dp'=4,'node'=16,'expert'=8] {'node','expert'}, dimensions={0} | all-to-all | bytes 3145728 | tf_op jit(solution)/shard_map/cond/branch_1_fun/all_to_all | solution.py:320
  103.5 1.6 gather.1.w_ref
  105.2 2.6 %forward.1 = bf16[4,4,96,512]{3,2,1,0:T(8,128)(2,1)S(1)} custom-call(s32[1]{0:T(128)} %bitcast.me_ref, bf16[16,8,48,128]{3,2,1,0:T(8,128)(2,1)S(1)} %bitcast.21, bf16[2,4,256,1024]{3,2,1,0:T(8,128)(2,1)S(1)} %gather.1.w_ref), custom_call_target="tpu_custom_call" | custom-call | tf_op jit(solution)/shard_map/forward/pallas_call | solution.py:255
  107.9 24.5 %all_to_all.20.part_ref = bf16[4,4,96,512]{3,2,1,0:T(8,128)(2,1)S(1)} all-to-all(bf16[4,4,96,512]{3,2,1,0:T(8,128)(2,1)S(1)} %forward.1), channel_id=1, replica_groups=mesh['dp'=4,'node'=16,'expert'=8] {'dp'}, dimensions={0} | all-to-all | bytes 3145728 | tf_op jit(solution)/shard_map/all_to_all | solution.py:341
  132.7 12.4 %all-gather = bf16[384,1152]{1,0:T(8,128)(2,1)S(1)} all-gather(bf16[96,1152]{1,0:T(8,128)(2,1)S(1)} %act.1), channel_id=2, replica_groups=mesh['dp'=4,'node'=16,'expert'=8] {'dp'}, dimensions={0}, use_global_device_ids=true | all-gather | bytes 1105920 | tf_op jit(solution)/shard_map/all_gather | solution.py:343
  145.1 1.3 backward.1
  146.5 39.6 %all_to_all.21.got_ref = bf16[128,32,128]{2,1,0:T(8,128)(2,1)S(1)} all-to-all(bf16[128,32,128]{2,1,0:T(8,128)(2,1)S(1)} %bitcast.13), channel_id=1, replica_groups=mesh['dp'=4,'node'=16,'expert'=8] {'node','expert'}, dimensions={0} | all-to-all | bytes 2097152 | tf_op jit(solution)/shard_map/all_to_all | solution.py:352
  186.1 1.2 combine.1
  187.3 3.1 %collective-permute-start.5 = (bf16[144,512]{1,0:T(8,128)(2,1)S(1)}, bf16[144,512]{1,0:T(8,128)(2,1)S(1)}, u32[]{:S(2)}, u32[]{:S(2)}) collective-permute-start(bf16[144,512]{1,0:T(8,128)(2,1)S(1)} %combine.1), channel_id=1, source_target_pairs={{0,0},{1,1},{130,2},{131,3},{260,4},{261,5},{390,6},{391,7},{2,128... | collective-permute-start | bytes 442376 | tf_op jit(solution)/shard_map/ppermute | solution.py:360
  190.4 14.7 %collective-permute-done.5 = bf16[144,512]{1,0:T(8,128)(2,1)S(1)} collective-permute-done((bf16[144,512]{1,0:T(8,128)(2,1)S(1)}, bf16[144,512]{1,0:T(8,128)(2,1)S(1)}, u32[]{:S(2)}, u32[]{:S(2)}) %collective-permute-start.5) | collective-permute-done | bytes 147488 | tf_op jit(solution)/shard_map/ppermute | solution.py:360
  (23 shorter events, 5.5 us)
Async XLA Ops:
  0.6 0.9 copy-start.2
  1.5 0.9 copy-start.3
  2.4 0.7 copy-start.4
  3.1 0.7 copy-start.5
  3.8 0.7 copy-start.6
  5.7 8.9 %all-to-all-start.1 = ((bf16[4,32,512]{2,1,0:T(8,128)(2,1)}), bf16[4,32,512]{2,1,0:T(8,128)(2,1)S(1)}, u32[]{:S(2)}, u32[]{:S(2)}) async-start(bf16[4,32,512]{2,1,0:T(8,128)(2,1)} %bitcast.4), calls=%async_computation.1 | async-start | bytes 262144 | tf_op jit(solution)/shard_map/all_to_all | solution.py:294
  9.9 14.5 %collective-permute-start = (bf16[144,512]{1,0:T(8,128)(2,1)S(1)}, bf16[144,512]{1,0:T(8,128)(2,1)S(1)}, u32[]{:S(2)}, u32[]{:S(2)}) collective-permute-start(bf16[144,512]{1,0:T(8,128)(2,1)S(1)} %get-tuple-element.24), channel_id=1, source_target_pairs={{0,0},{1,1},{2,130},{3,131},{4,260},{5,261},{6,390},{7,391},{128,2... | collective-permute-start | bytes 442376 | tf_op jit(solution)/shard_map/ppermute | solution.py:293
  14.6 11.6 %collective-permute-start.1 = (bf16[128,512]{1,0:T(8,128)(2,1)S(1)}, bf16[128,512]{1,0:T(8,128)(2,1)S(1)}, u32[]{:S(2)}, u32[]{:S(2)}) collective-permute-start(bf16[128,512]{1,0:T(8,128)(2,1)S(1)} %bitcast.17), channel_id=1, source_target_pairs={{0,0},{1,1},{2,130},{3,131},{4,260},{5,261},{6,390},{7,391},{128,2... | collective-permute-start | bytes 393224 | tf_op jit(solution)/shard_map/ppermute | solution.py:295
  19.4 1.6 copy-start
  21.0 1.6 copy-start.1
  26.2 77.3 %collective-permute-start.2 = (bf16[512,1024]{1,0:T(8,128)(2,1)}, bf16[512,1024]{1,0:T(8,128)(2,1)S(1)}, u32[]{:S(2)}, u32[]{:S(2)}) collective-permute-start(bf16[512,1024]{1,0:T(8,128)(2,1)} %get-tuple-element.33), channel_id=1, source_target_pairs={{0,128},{128,256},{256,384},{384,0},{1,129},{129,257},{257,385},{3... | collective-permute-start | bytes 3145736 | tf_op jit(solution)/shard_map/ppermute | solution.py:308
  28.1 75.4 %collective-permute-start.3 = (bf16[512,1024]{1,0:T(8,128)(2,1)}, bf16[512,1024]{1,0:T(8,128)(2,1)S(1)}, u32[]{:S(2)}, u32[]{:S(2)}) collective-permute-start(bf16[512,1024]{1,0:T(8,128)(2,1)} %get-tuple-element.34), channel_id=1, source_target_pairs={{0,256},{128,384},{256,0},{384,128},{1,257},{129,385},{257,1},{385... | collective-permute-start | bytes 3145736 | tf_op jit(solution)/shard_map/ppermute | solution.py:308
  34.0 69.5 %collective-permute-start.4 = (bf16[512,1024]{1,0:T(8,128)(2,1)}, bf16[512,1024]{1,0:T(8,128)(2,1)}, u32[]{:S(2)}, u32[]{:S(2)}) collective-permute-start(bf16[512,1024]{1,0:T(8,128)(2,1)} %get-tuple-element.35), channel_id=1, source_target_pairs={{0,384},{128,0},{256,128},{384,256},{1,385},{129,1},{257,129},{385... | collective-permute-start | bytes 3145736 | tf_op jit(solution)/shard_map/ppermute | solution.py:308
  39.4 1.4 copy-start.8
  103.5 1.7 copy-start.7
  187.3 17.8 %collective-permute-start.5 = (bf16[144,512]{1,0:T(8,128)(2,1)S(1)}, bf16[144,512]{1,0:T(8,128)(2,1)S(1)}, u32[]{:S(2)}, u32[]{:S(2)}) collective-permute-start(bf16[144,512]{1,0:T(8,128)(2,1)S(1)} %combine.1), channel_id=1, source_target_pairs={{0,0},{1,1},{130,2},{131,3},{260,4},{261,5},{390,6},{391,7},{2,128... | collective-permute-start | bytes 442376 | tf_op jit(solution)/shard_map/ppermute | solution.py:360

commit v3 on v2

v3 whole, which is shorter than its diff:
```python
import functools

import jax
import jax.numpy as jnp
from jax import lax
from jax.experimental import pallas as pl
from jax.experimental.pallas import tpu as pltpu
from jax.sharding import PartitionSpec as P

BF = jnp.bfloat16
F32 = jnp.float32
CAP = 6
TOK = 128
WID = 512
LANE = 128
PARAMS = pltpu.CompilerParams(vmem_limit_bytes=20 * 1024 * 1024)
HBM_PARAMS = pltpu.CompilerParams(vmem_limit_bytes=60 * 1024 * 1024)


def iota(shape, dim):
    return lax.broadcasted_iota(jnp.int32, shape, dim)


def split(index, base):
    high = jnp.floor((index + 0.5) * (1.0 / base))
    return high, index - high * base


def order_matrix(rows, columns, source):
    row = iota((rows, 1), 0).astype(F32)
    return jnp.where(iota((rows, columns), 1).astype(F32) == source(row), 1.0, 0.0).astype(BF)


def pack_source(row):
    expert, rest = split(row, 48)
    chunk, slot = split(rest, CAP)
    return chunk * 48 + slot * 8 + expert


def unpack_source(row):
    chunk, rest = split(row, 48)
    node, slot = split(rest, CAP)
    return node * 48 + chunk * CAP + slot


def collect_source(row):
    chunk, rest = split(row, 48)
    expert, slot = split(rest, CAP)
    return jnp.where(row < 192, expert * 32 + chunk * CAP + slot, jnp.where(row < 200, (row - 192) * 32 + 24, -1.0))


def reply_matrix():
    column = iota((1, 256), 1).astype(F32)
    chunk, rest = split(column, 48)
    node, slot = split(rest, CAP)
    target = jnp.where(column < 192, node * 32 + chunk * CAP + slot, jnp.where(column < 240, node * 32 + 24, -1.0))
    return jnp.where(iota((256, 256), 0).astype(F32) == target, 1.0, 0.0).astype(BF)


def dot(a, b):
    return jnp.dot(a, b, preferred_element_type=F32)


def dot_nt(a, b):
    return lax.dot_general(a, b, (((1,), (1,)), ((), ())), preferred_element_type=F32)


def dot_tn(a, b):
    return lax.dot_general(a, b, (((0,), (0,)), ((), ())), preferred_element_type=F32)


def named_rows(info):
    experts = iota((LANE, TOK), 0).astype(F32)
    named = jnp.zeros((LANE, TOK), F32)
    for j in range(4):
        named = named + jnp.where(info[j:j + 1, :] == experts, 1.0, 0.0)
    earlier = jnp.where(iota((TOK, TOK), 0) < iota((TOK, TOK), 1), 1.0, 0.0).astype(BF)
    return named, dot(named.astype(BF), earlier)


def load(pairs, sems):
    copies = [pltpu.make_async_copy(source, target, sems.at[i]) for i, (source, target) in enumerate(pairs)]
    for copy in copies:
        copy.start()
    for copy in copies:
        copy.wait()


def feature_part(me_ref, w_ref, k):
    start = pl.multiple_of(lax.rem(me_ref[0] + k, 4) * 1024, 1024)
    return w_ref.at[:, pl.ds(start, 1024)]


def prepare_kernel(shard_step, me_ref, x_hbm, dest_hbm, down_hbm, out_ref, far_ref, x_ref, dest_ref, sems):
    load(((dest_hbm, dest_ref), (x_hbm, x_ref), (feature_part(me_ref, down_hbm, 2), far_ref)), sems)
    dest = dest_ref[...]
    target = (dest // shard_step) * 32 + (dest % TOK) // 4
    pick = jnp.where(iota((TOK, TOK), 0) == target, 1.0, 0.0).astype(BF)
    out_ref[...] = dot(pick, x_ref[...]).astype(BF).reshape(4, 32, WID)


def split_kernel(me_ref, up_hbm, down_hbm, after_ref, right_ref, left_ref, own_ref, sems):
    load((
        (up_hbm, right_ref.at[:, :4096]), (up_hbm, left_ref.at[:, :4096]),
        (feature_part(me_ref, down_hbm, 1), right_ref.at[:, 4096:]),
        (feature_part(me_ref, down_hbm, 3), left_ref.at[:, 4096:]),
        (feature_part(me_ref, down_hbm, 0), own_ref),
    ), sems)


def pack_kernel(ids_ref, dy_ref, x_ref, out_ref, slots, rows):
    named, rank = named_rows(ids_ref[...].astype(F32))
    for s in range(CAP):
        slots[s] = jnp.where(rank == float(s), named, 0.0)
    token = iota((TOK, TOK), 0)
    order = jnp.where(iota((TOK, TOK), 1) == (token % 4) * 32 + token // 4, 1.0, 0.0).astype(BF)
    rows[:, :WID] = dy_ref[...]
    rows[:, WID:] = dot(order, x_ref[...].reshape(TOK, WID)).astype(BF)
    perm = order_matrix(384, 384, pack_source)
    for pair in range(8):
        halves = []
        for block in (2 * pair, 2 * pair + 1):
            pick = jnp.concatenate([slots[s, block * 8:block * 8 + 8, :] for s in range(CAP)], axis=0).astype(BF)
            got = dot(pick, rows[...]).astype(BF)
            halves.append(jnp.concatenate([got[:, a * LANE:(a + 1) * LANE] for a in range(8)], axis=0))
        sent = dot(perm, jnp.concatenate(halves, axis=1)).astype(BF)
        for h in range(2):
            out_ref[(2 * pair + h) * 8:(2 * pair + h) * 8 + 8] = sent[:, h * LANE:(h + 1) * LANE].reshape(8, 48, LANE)


def unpack_kernel(got_ref, dy_ref, x_ref):
    perm = order_matrix(384, 384, unpack_source)
    for pair in range(4):
        for half in range(2):
            both = jnp.concatenate(
                [got_ref[half * 8:half * 8 + 8, 2 * pair + b].reshape(384, LANE) for b in range(2)], axis=1
            )
            moved = dot(perm, both).astype(BF)
            rows = slice(half * 48, half * 48 + 48)
            for a in range(8):
                for b in range(2):
                    col = b * WID + (a % 4) * LANE
                    value = moved[a * 48:a * 48 + 48, b * LANE:(b + 1) * LANE]
                    if a < 4:
                        dy_ref[pair, rows, col:col + LANE] = value
                    else:
                        x_ref[rows, pair * 1024 + col:pair * 1024 + col + LANE] = value


def hidden_kernel(me_ref, dy_ref, own, left, far, right, out_ref):
    rows = dy_ref[...].reshape(384, 1024)
    for k, w in enumerate((own, left.at[:, 4096:], far, right.at[:, 4096:])):
        block = lax.rem(me_ref[0] - k + 4, 4)
        out_ref[:, block] = dot_nt(rows, w[...]).astype(BF).reshape(4, 96, 256)


def backward_kernel(me_ref, part_ref, x_ref, own, left, right, far_low, far_high, out_ref):
    me = me_ref[0]
    perm = reply_matrix()
    score = jnp.zeros((96, 1), F32)
    pieces = []
    for shift, weights in ((0, (own,)), (3, (left,)), (1, (right,)), (2, (far_low, far_high))):
        block = lax.rem(me + shift, 4)
        grad = part_ref[0, block].astype(F32)
        for s in range(1, 4):
            grad = grad + part_ref[s, block].astype(F32)
        pre = jnp.concatenate([dot_nt(x_ref[...], w[:, :4096]) for w in weights], axis=1)
        sig = jax.nn.sigmoid(pre)
        score = score + jnp.sum(pre * sig * grad, axis=1, keepdims=True)
        grad_pre = (grad * sig * (1.0 + pre * (1.0 - sig))).astype(BF)
        width = 256 // len(weights)
        pieces += [(grad_pre[:, i * width:(i + 1) * width], w) for i, w in enumerate(weights)]
    _, slot = split(iota((96, 1), 0).astype(F32), CAP)
    scores = jnp.where(iota((96, LANE), 1).astype(F32) == slot, score, 0.0).astype(BF)
    blank = jnp.zeros((16, LANE), BF)
    for pair in range(4):
        total = sum(dot(grad_pre, w[:, pair * 1024:pair * 1024 + 1024]) for grad_pre, w in pieces).astype(BF)
        for half in range(2):
            rows = slice(half * 48, half * 48 + 48)
            stacks = []
            for b in range(2):
                parts = [total[rows, b * WID + c * LANE:b * WID + (c + 1) * LANE] for c in range(4)]
                stacks.append(jnp.concatenate(parts + [scores[rows], blank], axis=0))
            sent = dot(perm, jnp.concatenate(stacks, axis=1)).astype(BF)
            for b in range(2):
                out_ref[half * 8:half * 8 + 8, 2 * pair + b] = sent[:, b * LANE:(b + 1) * LANE].reshape(8, 32, LANE)


def combine_kernel(got_ref, ids_ref, w_ref, out_ref, score_ref, rows, scores):
    weights = w_ref[...]
    high = weights.astype(BF).astype(F32)
    middle = (weights - high).astype(BF).astype(F32)
    low = weights - high - middle
    ids = ids_ref[...].astype(F32)
    info_rows = jnp.concatenate([ids, high, middle, low], axis=0).astype(BF)
    named, rank_rows = named_rows(ids)
    eye = jnp.where(iota((TOK, TOK), 0) == iota((TOK, TOK), 1), 1.0, 0.0).astype(BF)
    rank = dot_tn(rank_rows.astype(BF), eye)
    info = dot_tn(info_rows, eye[:16])
    perm = order_matrix(208, 256, collect_source)
    for pair in range(8):
        both = jnp.concatenate(
            [got_ref[(2 * pair + h) * 8:(2 * pair + h) * 8 + 8].reshape(256, LANE) for h in range(2)], axis=1
        )
        moved = dot(perm, both)
        for h in range(2):
            block = 2 * pair + h
            half = moved[:, h * LANE:(h + 1) * LANE]
            scores[block * 8:block * 8 + 8] = half[192:200]
            for c in range(4):
                rows[block * 48:block * 48 + 48, c * LANE:(c + 1) * LANE] = half[c * 48:c * 48 + 48].astype(BF)
    lanes = iota((TOK, LANE), 1).astype(F32)
    wide = iota((TOK, 128 * CAP), 1).astype(F32)
    coefs = [jnp.zeros((TOK, 128 * CAP), F32) for _ in range(3)]
    table = scores[...].astype(BF)
    back = jnp.zeros((TOK, LANE), F32)
    for j in range(4):
        expert = info[:, j:j + 1]
        mine = expert == lanes
        slot = jnp.sum(jnp.where(mine, rank, 0.0), axis=1, keepdims=True)
        here = wide == expert * float(CAP) + slot
        for p in range(3):
            coefs[p] = jnp.where(here, info[:, 4 + 4 * p + j:5 + 4 * p + j], coefs[p])
        line = dot(jnp.where(mine, 1.0, 0.0).astype(BF), table)
        value = jnp.sum(jnp.where(lanes == slot, line, 0.0), axis=1, keepdims=True)
        back = jnp.where(lanes == float(j), value, back)
    values = rows[...]
    total = dot(coefs[0].astype(BF), values) + (dot(coefs[1].astype(BF), values) + dot(coefs[2].astype(BF), values))
    out_ref[...] = total.astype(BF)
    score_ref[...] = dot_tn(back.astype(BF), eye)[:4].astype(BF)


VM = pl.BlockSpec(memory_space=pltpu.VMEM)
SM = pl.BlockSpec(memory_space=pltpu.SMEM)
HBM = pl.BlockSpec(memory_space=pltpu.HBM)


def call(kernel, out_shape, args, in_specs=None, scratch=(), name=None, out_spec=VM, params=PARAMS):
    return pl.pallas_call(
        kernel,
        out_shape=out_shape,
        in_specs=in_specs or [VM] * len(args),
        out_specs=jax.tree.map(lambda _: out_spec, out_shape),
        scratch_shapes=list(scratch),
        compiler_params=params,
        name=name,
    )(*args)


def struct(shape):
    return jax.ShapeDtypeStruct(shape, BF)


def shards(x_rollout, dest, route_ids, route_weights, cotangent, w_up, w_down):
    dp = lax.axis_size("dp")
    node = lax.axis_size("node")
    group = lax.axis_size("expert")
    me = lax.axis_index("dp")
    me_arr = me.reshape(1).astype(jnp.int32)
    plane = ("node", "expert")
    ids = route_ids.T

    up = w_up[0]
    to_right, to_left, to_far = ([(i, (i + k) % dp) for i in range(dp)] for k in (1, dp - 1, 2))
    down = w_down[0]
    sorted_x, sent_far = call(
        functools.partial(prepare_kernel, node * TOK),
        (struct((4, 32, WID)), struct((256, 1024))),
        (me_arr, x_rollout, dest.reshape(1, TOK), down),
        in_specs=[SM] + [HBM] * 3,
        scratch=(pltpu.VMEM((TOK, WID), BF), pltpu.VMEM((1, TOK), jnp.int32), pltpu.SemaphoreType.DMA((3,))),
        params=HBM_PARAMS,
        name="prepare",
    )
    far = lax.ppermute(sent_far, "dp", to_far)
    arrived = lax.all_to_all(sorted_x, "dp", split_axis=0, concat_axis=0, tiled=True)
    sent = call(
        split_kernel,
        [struct((256, 5120)), struct((256, 5120)), struct((256, 1024))],
        (me_arr, up, down, sorted_x),
        in_specs=[SM, HBM, HBM, pl.BlockSpec(memory_space=pl.ANY)],
        scratch=(pltpu.SemaphoreType.DMA((5,)),),
        params=HBM_PARAMS,
        name="split",
    )
    arrived, sent = lax.optimization_barrier((arrived, sent))
    left = lax.ppermute(sent[0], "dp", to_right)
    right = lax.ppermute(sent[1], "dp", to_left)

    def exchange(ids, dy, x):
        send = call(
            pack_kernel,
            struct((128, 48, LANE)),
            (ids, dy, x),
            scratch=(pltpu.VMEM((CAP, TOK, LANE), F32), pltpu.VMEM((TOK, 2 * WID), BF)),
            name="pack",
        )
        return lax.all_to_all(send, plane, split_axis=0, concat_axis=0, tiled=True)

    got = lax.cond(me >= 0, exchange, lambda ids, dy, x: jnp.zeros((128, 48, LANE), BF), ids, cotangent, arrived)
    got, left, right, far = lax.optimization_barrier((got, left, right, far))
    far_low = lax.ppermute(left[:128, :4096], "dp", to_right)
    far_high = lax.ppermute(right[128:, :4096], "dp", to_left)
    rows_dy, rows_x = call(
        unpack_kernel,
        (struct((4, 96, 1024)), struct((96, 4096))),
        (got.reshape(node, group, 48, LANE),),
        name="unpack",
    )
    rows_dy = lax.all_to_all(rows_dy, "dp", split_axis=0, concat_axis=0, tiled=True)
    part = call(
        hidden_kernel,
        struct((4, 4, 96, 256)),
        (me_arr, rows_dy, sent[2], left, far, right),
        in_specs=[SM] + [VM] * 5,
        name="hidden",
    )
    part = lax.all_to_all(part, "dp", split_axis=0, concat_axis=0, tiled=True)
    reply = call(
        backward_kernel,
        struct((node, group, 32, LANE)),
        (me_arr, part, rows_x, up, left, right, far_low, far_high),
        in_specs=[SM] + [VM] * 7,
        name="backward",
    )
    back = lax.all_to_all(reply.reshape(128, 32, LANE), plane, split_axis=0, concat_axis=0, tiled=True)
    grads, scores = call(
        combine_kernel,
        (struct((TOK, WID)), struct((4, TOK))),
        (back, ids, route_weights.T),
        scratch=(pltpu.VMEM((128 * CAP, WID), BF), pltpu.VMEM((LANE, LANE), F32)),
        name="combine",
    )
    return grads, scores.T


def solution(mesh):
    in_specs = (
        P(("dp", "node"), "expert"),
        P(("dp", "node")),
        P(("dp", "node"), None),
        P(("dp", "node"), None),
        P(("dp", "node"), "expert"),
        P(("node", "expert"), "dp", None),
        P(("node", "expert"), "dp", None),
    )
    out_specs = (P(("dp", "node"), "expert"), P(("dp", "node"), None))
    return jax.shard_map(shards, mesh=mesh, in_specs=in_specs, out_specs=out_specs, check_vma=False)
```

time: 207 us -> 199 us (0.961)
  the two profiles are of different devices: /device:TPU:15 before, /device:TPU:1 now
where the time goes in v3:
time: 199 us; the launch traced here: 198 us
  blocking collectives  114 us (57%)
  starting transfers between devices  28.9 us (15%)
  Pallas kernels  23.7 us (12%)
  waiting for transfers between devices  19.3 us (10%)
  local copies, waits for them, and re-layouts  11 us (6%)
    all_to_all x1, blocking collectives, exchange(): return lax.all_to_all(send, plane, split_axis=0, concat_axis=0, tiled=True)  60.4 us
    all_to_all x1, blocking collectives, shards(): lax.all_to_all(reply.reshape(128, 32, LANE), plane, split_axis=0, concat_...  54 us
    pallas_call x7, Pallas kernels, call(): pl.pallas_call(kernel, out_shape=out_shape, in_specs=in_specs or [VM] * l...  23.7 us
    ppermute x1, waiting for transfers between devices, shards(): far_high = lax.ppermute(right[128:, :4096], 'dp', to_left)  11.2 us
    unnamed x22, local copies, waits for them, and re-layouts  7.64 us
    all_to_all x1, waiting for transfers between devices, shards(): part = lax.all_to_all(part, 'dp', split_axis=0, concat_axis=0, tiled=True)  7.1 us
    all_to_all x1, starting transfers between devices, shards(): lax.all_to_all(sorted_x, 'dp', split_axis=0, concat_axis=0, tiled=True)  4.85 us
    ppermute x1, starting transfers between devices, shards(): far_high = lax.ppermute(right[128:, :4096], 'dp', to_left)  4.54 us
  transfers between devices with their start and end apart: 8, of which 3 were waited for; matrix products, arithmetic and copies ran while one was open for 2% of the time, Pallas kernels for 5%

profile of v3, /device:TPU:1, one launch (start us, length us, event | category | flops | bytes accessed | tf_op | source)
XLA Modules:
  0.0 198.2 jit_solution(5516746263137970021)
XLA Ops:
  0.6 2.0 %prepare.1 = (bf16[4,32,512]{2,1,0:T(8,128)(2,1)}, bf16[256,1024]{1,0:T(8,128)(2,1)}) custom-call(s32[1]{0:T(128)} %bitcast.me_ref, bf16[128,512]{1,0:T(8,128)(2,1)} %x_hbm.1, s32[1,128]{1,0:T(1,128)} %bitcast.18, bf16[256,4096]{1,0:T(8,128)(2,1)} %bitcast.13), custom_call_target="tpu_custom_call" | custom-call | tf_op jit(solution)/shard_map/prepare/pallas_call | solution.py:239
  2.6 4.9 %all-to-all-start.1 = ((bf16[4,32,512]{2,1,0:T(8,128)(2,1)}), bf16[4,32,512]{2,1,0:T(8,128)(2,1)S(1)}, u32[]{:S(2)}, u32[]{:S(2)}) async-start(bf16[4,32,512]{2,1,0:T(8,128)(2,1)} %get-tuple-element.31.after_ref), calls=%async_computation.1 | async-start | bytes 262144 | tf_op jit(solution)/shard_map/all_to_all | solution.py:276
  7.5 5.2 %split.1 = (bf16[256,5120]{1,0:T(8,128)(2,1)}, bf16[256,5120]{1,0:T(8,128)(2,1)}, bf16[256,1024]{1,0:T(8,128)(2,1)}) custom-call(s32[1]{0:T(128)} %bitcast.me_ref, bf16[256,4096]{1,0:T(8,128)(2,1)} %bitcast.9, bf16[256,4096]{1,0:T(8,128)(2,1)} %bitcast.14, bf16[4,32,512]{2,1,0:T(8,128)(2,1)} %get-tuple-element.31.after_ref), custom_call_target="tpu_custom_call" | custom-call | tf_op jit(solution)/shard_map/split/pallas_call | solution.py:239
  12.7 3.4 %collective-permute-start = (bf16[256,5120]{1,0:T(8,128)(2,1)}, bf16[256,5120]{1,0:T(8,128)(2,1)S(1)}, u32[]{:S(2)}, u32[]{:S(2)}) collective-permute-start(bf16[256,5120]{1,0:T(8,128)(2,1)} %get-tuple-element.36), channel_id=1, source_target_pairs={{0,128},{128,256},{256,384},{384,0},{1,129},{129,257},{257,385},{3... | collective-permute-start | bytes 7864328 | tf_op jit(solution)/shard_map/ppermute | solution.py:287
  16.1 3.1 %collective-permute-start.1 = (bf16[256,5120]{1,0:T(8,128)(2,1)}, bf16[256,5120]{1,0:T(8,128)(2,1)}, u32[]{:S(2)}, u32[]{:S(2)}) collective-permute-start(bf16[256,5120]{1,0:T(8,128)(2,1)} %get-tuple-element.37), channel_id=1, source_target_pairs={{0,384},{128,0},{256,128},{384,256},{1,385},{129,1},{257,129},{385... | collective-permute-start | bytes 7864328 | tf_op jit(solution)/shard_map/ppermute | solution.py:288
  19.2 3.7 %collective-permute-start.2 = (bf16[256,1024]{1,0:T(8,128)(2,1)}, bf16[256,1024]{1,0:T(8,128)(2,1)S(1)}, u32[]{:S(2)}, u32[]{:S(2)}) collective-permute-start(bf16[256,1024]{1,0:T(8,128)(2,1)} %get-tuple-element.38), channel_id=1, source_target_pairs={{0,256},{128,384},{256,0},{384,128},{1,257},{129,385},{257,1},{385... | collective-permute-start | bytes 1572872 | tf_op jit(solution)/shard_map/ppermute | solution.py:275
  22.9 62.7 %conditional.1 = (bf16[128,48,128]{2,1,0:T(8,128)(2,1)}) conditional(s32[]{:T(128)} %convert_element_type.3, () %tuple.16, (s32[4,128]{1,0:T(4,128)S(1)}, bf16[128,512]{1,0:T(8,128)(2,1)S(1)}, bf16[4,32,512]{2,1,0:T(8,128)(2,1)S(1)}) %tuple.24), branch_computations={%region_0.0_spmd, %region_1.0_spmd} | conditional | bytes 3145736 | solution.py:300
  22.9 2.3 %pack.1 = bf16[128,48,128]{2,1,0:T(8,128)(2,1)S(1)} custom-call(s32[4,128]{1,0:T(4,128)S(1)} %get-tuple-element.2.ids_ref, bf16[128,512]{1,0:T(8,128)(2,1)S(1)} %get-tuple-element.49.dy_ref, bf16[4,32,512]{2,1,0:T(8,128)(2,1)S(1)} %get-tuple-element.11.x_ref), custom_call_target="tpu_custom_call" | custom-call | tf_op jit(solution)/shard_map/cond/branch_1_fun/pack/pallas_call | solution.py:239
  25.2 60.4 %all_to_all.24 = bf16[128,48,128]{2,1,0:T(8,128)(2,1)} all-to-all(bf16[128,48,128]{2,1,0:T(8,128)(2,1)S(1)} %pack.1), channel_id=1, replica_groups=mesh['dp'=4,'node'=16,'expert'=8] {'node','expert'}, dimensions={0} | all-to-all | bytes 3145728 | tf_op jit(solution)/shard_map/cond/branch_1_fun/all_to_all | solution.py:298
  85.6 2.6 %unpack.1 = (bf16[4,96,1024]{2,1,0:T(8,128)(2,1)S(1)}, bf16[96,4096]{1,0:T(8,128)(2,1)S(1)}) custom-call(bf16[16,8,48,128]{3,2,1,0:T(8,128)(2,1)} %bitcast.15), custom_call_target="tpu_custom_call" | custom-call | tf_op jit(solution)/shard_map/unpack/pallas_call | solution.py:239
  90.1 3.5 %all-to-all-start.2 = ((bf16[4,96,1024]{2,1,0:T(8,128)(2,1)}), bf16[4,96,1024]{2,1,0:T(8,128)(2,1)S(1)}, u32[]{:S(2)}, u32[]{:S(2)}) async-start(bf16[4,96,1024]{2,1,0:T(8,128)(2,1)} %copy-done.4), calls=%async_computation.2 | async-start | bytes 1572864 | tf_op jit(solution)/shard_map/all_to_all | solution.py:310
  93.6 1.1 slice.6
  94.6 2.3 %slice.7 = bf16[128,4096]{1,0:T(8,128)(2,1)} slice(bf16[256,5120]{1,0:T(8,128)(2,1)} %collective-permute-done.1.right), slice={[128:256], [0:4096]} | slice | bytes 2097152 | tf_op jit(solution)/shard_map/slice | solution.py:303
  96.9 4.5 %collective-permute-start.4 = (bf16[128,4096]{1,0:T(8,128)(2,1)}, bf16[128,4096]{1,0:T(8,128)(2,1)}, u32[]{:S(2)}, u32[]{:S(2)}) collective-permute-start(bf16[128,4096]{1,0:T(8,128)(2,1)} %slice.7), channel_id=1, source_target_pairs={{0,384},{128,0},{256,128},{384,256},{1,385},{129,1},{257,129},{385... | collective-permute-start | bytes 3145736 | tf_op jit(solution)/shard_map/ppermute | solution.py:303
  101.5 1.9 collective-permute-start.3
  105.5 2.7 %hidden.1 = bf16[4,4,96,256]{3,2,1,0:T(8,128)(2,1)S(1)} custom-call(s32[1]{0:T(128)} %bitcast.me_ref, bf16[4,96,1024]{2,1,0:T(8,128)(2,1)S(1)} %all-to-all-done.2.dy_ref, bf16[256,1024]{1,0:T(8,128)(2,1)S(1)} %copy-done.5, bf16[256,5120]{1,0:T(8,128)(2,1)S(1)} %collective-permute-done.left, bf16[256,1024]{1,0:T(8,128)(2,1)S(1)} %copy-done.7, ...), custom_call_target="tpu_custom_call" | custom-call | tf_op jit(solution)/shard_map/hidden/pallas_call | solution.py:239
  109.2 3.9 %all-to-all-start.3 = ((bf16[4,4,96,256]{3,2,1,0:T(8,128)(2,1)}), bf16[4,4,96,256]{3,2,1,0:T(8,128)(2,1)S(1)}, u32[]{:S(2)}, u32[]{:S(2)}) async-start(bf16[4,4,96,256]{3,2,1,0:T(8,128)(2,1)} %copy-done.1), calls=%async_computation.3 | async-start | bytes 1572864 | tf_op jit(solution)/shard_map/all_to_all | solution.py:318
  113.2 11.2 %collective-permute-done.4.far_high = bf16[128,4096]{1,0:T(8,128)(2,1)} collective-permute-done((bf16[128,4096]{1,0:T(8,128)(2,1)}, bf16[128,4096]{1,0:T(8,128)(2,1)}, u32[]{:S(2)}, u32[]{:S(2)}) %collective-permute-start.4) | collective-permute-done | bytes 1048608 | tf_op jit(solution)/shard_map/ppermute | solution.py:303
  125.4 7.1 %all-to-all-done.3.part_ref = bf16[4,4,96,256]{3,2,1,0:T(8,128)(2,1)S(1)} async-done(((bf16[4,4,96,256]{3,2,1,0:T(8,128)(2,1)}), bf16[4,4,96,256]{3,2,1,0:T(8,128)(2,1)S(1)}, u32[]{:S(2)}, u32[]{:S(2)}) %all-to-all-start.3) | async-done | bytes 786464 | tf_op jit(solution)/shard_map/all_to_all | solution.py:318
  132.5 1.6 copy-done
  134.1 1.1 copy-done.3
  135.2 7.1 %backward.1 = bf16[16,8,32,128]{3,2,1,0:T(8,128)(2,1)S(1)} custom-call(s32[1]{0:T(128)} %bitcast.me_ref, bf16[4,4,96,256]{3,2,1,0:T(8,128)(2,1)S(1)} %all-to-all-done.3.part_ref, bf16[96,4096]{1,0:T(8,128)(2,1)S(1)} %copy-done.3, bf16[256,4096]{1,0:T(8,128)(2,1)S(1)} %bitcast.10, bf16[256,5120]{1,0:T(8,128)(2,1)S(1)} %collective-permute-done.left, ...), custom_call_target="tpu_custom_call" | custom-call | tf_op jit(solution)/shard_map/backward/pallas_call | solution.py:239
  142.3 54.0 %all_to_all.25.got_ref = bf16[128,32,128]{2,1,0:T(8,128)(2,1)S(1)} all-to-all(bf16[128,32,128]{2,1,0:T(8,128)(2,1)S(1)} %bitcast.11), channel_id=1, replica_groups=mesh['dp'=4,'node'=16,'expert'=8] {'node','expert'}, dimensions={0} | all-to-all | bytes 2097152 | tf_op jit(solution)/shard_map/all_to_all | solution.py:326
  196.3 1.9 combine.1
  (26 shorter events, 6.0 us)
Async XLA Ops:
  2.6 10.0 %all-to-all-start.1 = ((bf16[4,32,512]{2,1,0:T(8,128)(2,1)}), bf16[4,32,512]{2,1,0:T(8,128)(2,1)S(1)}, u32[]{:S(2)}, u32[]{:S(2)}) async-start(bf16[4,32,512]{2,1,0:T(8,128)(2,1)} %get-tuple-element.31.after_ref), calls=%async_computation.1 | async-start | bytes 262144 | tf_op jit(solution)/shard_map/all_to_all | solution.py:276
  7.5 15.4 %copy-start.9 = (bf16[128,512]{1,0:T(8,128)(2,1)S(1)}, bf16[128,512]{1,0:T(8,128)(2,1)}, u32[]{:S(2)}) copy-start(bf16[128,512]{1,0:T(8,128)(2,1)} %param.13) | copy-start | bytes 393220
  7.5 15.4 %copy-start.10 = (s32[128,4]{0,1:T(4,128)S(1)}, s32[128,4]{0,1:T(4,128)}, u32[]{:S(2)}) copy-start(s32[128,4]{0,1:T(4,128)} %param.11) | copy-start | bytes 6148
  12.7 72.9 %collective-permute-start = (bf16[256,5120]{1,0:T(8,128)(2,1)}, bf16[256,5120]{1,0:T(8,128)(2,1)S(1)}, u32[]{:S(2)}, u32[]{:S(2)}) collective-permute-start(bf16[256,5120]{1,0:T(8,128)(2,1)} %get-tuple-element.36), channel_id=1, source_target_pairs={{0,128},{128,256},{256,384},{384,0},{1,129},{129,257},{257,385},{3... | collective-permute-start | bytes 7864328 | tf_op jit(solution)/shard_map/ppermute | solution.py:287
  16.1 69.5 %collective-permute-start.1 = (bf16[256,5120]{1,0:T(8,128)(2,1)}, bf16[256,5120]{1,0:T(8,128)(2,1)}, u32[]{:S(2)}, u32[]{:S(2)}) collective-permute-start(bf16[256,5120]{1,0:T(8,128)(2,1)} %get-tuple-element.37), channel_id=1, source_target_pairs={{0,384},{128,0},{256,128},{384,256},{1,385},{129,1},{257,129},{385... | collective-permute-start | bytes 7864328 | tf_op jit(solution)/shard_map/ppermute | solution.py:288
  19.2 66.4 %collective-permute-start.2 = (bf16[256,1024]{1,0:T(8,128)(2,1)}, bf16[256,1024]{1,0:T(8,128)(2,1)S(1)}, u32[]{:S(2)}, u32[]{:S(2)}) collective-permute-start(bf16[256,1024]{1,0:T(8,128)(2,1)} %get-tuple-element.38), channel_id=1, source_target_pairs={{0,256},{128,384},{256,0},{384,128},{1,257},{129,385},{257,1},{385... | collective-permute-start | bytes 1572872 | tf_op jit(solution)/shard_map/ppermute | solution.py:275
  85.6 4.5 %copy-start.6 = (bf16[256,1024]{1,0:T(8,128)(2,1)}, bf16[256,1024]{1,0:T(8,128)(2,1)S(1)}, u32[]{:S(2)}) copy-start(bf16[256,1024]{1,0:T(8,128)(2,1)S(1)} %collective-permute-done.2.far) | copy-start | bytes 1572868
  88.2 0.9 copy-start.2
  89.1 1.0 copy-start.4
  90.1 13.4 %all-to-all-start.2 = ((bf16[4,96,1024]{2,1,0:T(8,128)(2,1)}), bf16[4,96,1024]{2,1,0:T(8,128)(2,1)S(1)}, u32[]{:S(2)}, u32[]{:S(2)}) async-start(bf16[4,96,1024]{2,1,0:T(8,128)(2,1)} %copy-done.4), calls=%async_computation.2 | async-start | bytes 1572864 | tf_op jit(solution)/shard_map/all_to_all | solution.py:310
  96.9 27.4 %collective-permute-start.4 = (bf16[128,4096]{1,0:T(8,128)(2,1)}, bf16[128,4096]{1,0:T(8,128)(2,1)}, u32[]{:S(2)}, u32[]{:S(2)}) collective-permute-start(bf16[128,4096]{1,0:T(8,128)(2,1)} %slice.7), channel_id=1, source_target_pairs={{0,384},{128,0},{256,128},{384,256},{1,385},{129,1},{257,129},{385... | collective-permute-start | bytes 3145736 | tf_op jit(solution)/shard_map/ppermute | solution.py:303
  101.5 23.9 %collective-permute-start.3 = (bf16[128,4096]{1,0:T(8,128)(2,1)}, bf16[128,4096]{1,0:T(8,128)(2,1)}, u32[]{:S(2)}, u32[]{:S(2)}) collective-permute-start(bf16[128,4096]{1,0:T(8,128)(2,1)} %slice.6), channel_id=1, source_target_pairs={{0,128},{128,256},{256,384},{384,0},{1,129},{129,257},{257,385},{3... | collective-permute-start | bytes 3145736 | tf_op jit(solution)/shard_map/ppermute | solution.py:302
  103.4 1.0 copy-start.5
  104.5 1.0 copy-start.7
  108.3 1.0 copy-start.1
  109.2 23.3 %all-to-all-start.3 = ((bf16[4,4,96,256]{3,2,1,0:T(8,128)(2,1)}), bf16[4,4,96,256]{3,2,1,0:T(8,128)(2,1)S(1)}, u32[]{:S(2)}, u32[]{:S(2)}) async-start(bf16[4,4,96,256]{3,2,1,0:T(8,128)(2,1)} %copy-done.1), calls=%async_computation.3 | async-start | bytes 1572864 | tf_op jit(solution)/shard_map/all_to_all | solution.py:318
  132.5 1.6 copy-start
  134.1 1.1 copy-start.3
  142.3 54.0 %copy-start.8 = (f32[128,4]{0,1:T(4,128)S(1)}, f32[128,4]{0,1:T(4,128)}, u32[]{:S(2)}) copy-start(f32[128,4]{0,1:T(4,128)} %param.12) | copy-start | bytes 6148

commit v4 on v3

--- a/solution.py
+++ b/solution.py
@@ -295,18 +295,21 @@
             scratch=(pltpu.VMEM((CAP, TOK, LANE), F32), pltpu.VMEM((TOK, 2 * WID), BF)),
             name="pack",
         )
-        return lax.all_to_all(send, plane, split_axis=0, concat_axis=0, tiled=True)
-
-    got = lax.cond(me >= 0, exchange, lambda ids, dy, x: jnp.zeros((128, 48, LANE), BF), ids, cotangent, arrived)
-    got, left, right, far = lax.optimization_barrier((got, left, right, far))
+        got = lax.all_to_all(send, plane, split_axis=0, concat_axis=0, tiled=True)
+        return call(
+            unpack_kernel,
+            (struct((4, 96, 1024)), struct((96, 4096))),
+            (got.reshape(node, group, 48, LANE),),
+            name="unpack",
+        )
+
+    def nothing(ids, dy, x):
+        return jnp.zeros((4, 96, 1024), BF), jnp.zeros((96, 4096), BF)
+
+    rows_dy, rows_x = lax.cond(me >= 0, exchange, nothing, ids, cotangent, arrived)
+    rows_dy, rows_x, left, right, far = lax.optimization_barrier((rows_dy, rows_x, left, right, far))
     far_low = lax.ppermute(left[:128, :4096], "dp", to_right)
     far_high = lax.ppermute(right[128:, :4096], "dp", to_left)
-    rows_dy, rows_x = call(
-        unpack_kernel,
-        (struct((4, 96, 1024)), struct((96, 4096))),
-        (got.reshape(node, group, 48, LANE),),
-        name="unpack",
-    )
     rows_dy = lax.all_to_all(rows_dy, "dp", split_axis=0, concat_axis=0, tiled=True)
     part = call(
         hidden_kernel,

time: 199 us -> 195 us (0.980)
  blocking collectives: 114 us -> 110 us
  waiting for transfers between devices: 19.3 us -> 21.8 us
  local copies, waits for them, and re-layouts: 11 us -> 8.74 us
    all_to_all x1, blocking collectives: 54 us -> 49.8 us  [shards(): lax.all_to_all(reply.reshape(128, 32, LANE), plane, split_axis=0, concat_...]
    unnamed x22 -> x16, local copies, waits for them, and re-layouts: 7.64 us -> 5.38 us
  transfers between devices with their start and end apart: 8 -> 8, of which waited for: 3 -> 4; matrix products, arithmetic and copies ran while one was open for 2% -> 2% of each run, Pallas kernels for 5% -> 6%
where the time goes in v4:
time: 195 us; the launch traced here: 194 us
  blocking collectives  110 us (56%)
  starting transfers between devices  28.7 us (15%)
  Pallas kernels  23.6 us (12%)
  waiting for transfers between devices  21.8 us (11%)
  local copies, waits for them, and re-layouts  8.74 us (4%)
    all_to_all x1, blocking collectives, exchange(): got = lax.all_to_all(send, plane, split_axis=0, concat_axis=0, tiled=True)  60.3 us
    all_to_all x1, blocking collectives, shards(): lax.all_to_all(reply.reshape(128, 32, LANE), plane, split_axis=0, concat_...  49.8 us
    pallas_call x7, Pallas kernels, call(): pl.pallas_call(kernel, out_shape=out_shape, in_specs=in_specs or [VM] * l...  23.6 us
    ppermute x1, waiting for transfers between devices, shards(): far_high = lax.ppermute(right[128:, :4096], 'dp', to_left)  11.7 us
    all_to_all x1, waiting for transfers between devices, shards(): part = lax.all_to_all(part, 'dp', split_axis=0, concat_axis=0, tiled=True)  7.1 us
    unnamed x16, local copies, waits for them, and re-layouts  5.38 us
    all_to_all x1, starting transfers between devices, shards(): lax.all_to_all(sorted_x, 'dp', split_axis=0, concat_axis=0, tiled=True)  4.99 us
    ppermute x1, starting transfers between devices, shards(): far_high = lax.ppermute(right[128:, :4096], 'dp', to_left)  4.54 us
  transfers between devices with their start and end apart: 8, of which 4 were waited for; matrix products, arithmetic and copies ran while one was open for 2% of the time, Pallas kernels for 6%

profile of v4, /device:TPU:1, one launch (start us, length us, event | category | flops | bytes accessed | tf_op | source)
XLA Modules:
  0.0 193.8 jit_solution(18333181453458237160)
XLA Ops:
  0.6 2.0 %prepare.1 = (bf16[4,32,512]{2,1,0:T(8,128)(2,1)}, bf16[256,1024]{1,0:T(8,128)(2,1)}) custom-call(s32[1]{0:T(128)} %bitcast.1.me_ref, bf16[128,512]{1,0:T(8,128)(2,1)} %x_hbm.1, s32[1,128]{1,0:T(1,128)} %bitcast.18, bf16[256,4096]{1,0:T(8,128)(2,1)} %bitcast.14), custom_call_target="tpu_custom_call" | custom-call | tf_op jit(solution)/shard_map/prepare/pallas_call | solution.py:239
  2.7 5.0 %all-to-all-start.1 = ((bf16[4,32,512]{2,1,0:T(8,128)(2,1)}), bf16[4,32,512]{2,1,0:T(8,128)(2,1)S(1)}, u32[]{:S(2)}, u32[]{:S(2)}) async-start(bf16[4,32,512]{2,1,0:T(8,128)(2,1)} %get-tuple-element.29.after_ref), calls=%async_computation.1 | async-start | bytes 262144 | tf_op jit(solution)/shard_map/all_to_all | solution.py:276
  7.6 5.2 %split.1 = (bf16[256,5120]{1,0:T(8,128)(2,1)}, bf16[256,5120]{1,0:T(8,128)(2,1)}, bf16[256,1024]{1,0:T(8,128)(2,1)}) custom-call(s32[1]{0:T(128)} %bitcast.1.me_ref, bf16[256,4096]{1,0:T(8,128)(2,1)} %bitcast.9, bf16[256,4096]{1,0:T(8,128)(2,1)} %bitcast.15, bf16[4,32,512]{2,1,0:T(8,128)(2,1)} %get-tuple-element.29.after_ref), custom_call_target="tpu_custom_call" | custom-call | tf_op jit(solution)/shard_map/split/pallas_call | solution.py:239
  12.8 3.4 %collective-permute-start = (bf16[256,5120]{1,0:T(8,128)(2,1)}, bf16[256,5120]{1,0:T(8,128)(2,1)S(1)}, u32[]{:S(2)}, u32[]{:S(2)}) collective-permute-start(bf16[256,5120]{1,0:T(8,128)(2,1)} %get-tuple-element.36), channel_id=1, source_target_pairs={{0,128},{128,256},{256,384},{384,0},{1,129},{129,257},{257,385},{3... | collective-permute-start | bytes 7864328 | tf_op jit(solution)/shard_map/ppermute | solution.py:287
  16.2 3.1 %collective-permute-start.1 = (bf16[256,5120]{1,0:T(8,128)(2,1)}, bf16[256,5120]{1,0:T(8,128)(2,1)}, u32[]{:S(2)}, u32[]{:S(2)}) collective-permute-start(bf16[256,5120]{1,0:T(8,128)(2,1)} %get-tuple-element.37), channel_id=1, source_target_pairs={{0,384},{128,0},{256,128},{384,256},{1,385},{129,1},{257,129},{385... | collective-permute-start | bytes 7864328 | tf_op jit(solution)/shard_map/ppermute | solution.py:288
  19.3 3.7 %collective-permute-start.2 = (bf16[256,1024]{1,0:T(8,128)(2,1)}, bf16[256,1024]{1,0:T(8,128)(2,1)S(1)}, u32[]{:S(2)}, u32[]{:S(2)}) collective-permute-start(bf16[256,1024]{1,0:T(8,128)(2,1)} %get-tuple-element.38), channel_id=1, source_target_pairs={{0,256},{128,384},{256,0},{384,128},{1,257},{129,385},{257,1},{385... | collective-permute-start | bytes 1572872 | tf_op jit(solution)/shard_map/ppermute | solution.py:275
  23.0 64.8 %conditional.1 = ((bf16[4,96,1024]{2,1,0:T(8,128)(2,1)}, bf16[96,4096]{1,0:T(8,128)(2,1)})) conditional(s32[]{:T(128)} %convert_element_type.3, () %tuple.17, (s32[4,128]{1,0:T(4,128)S(1)}, bf16[128,512]{1,0:T(8,128)(2,1)S(1)}, bf16[4,32,512]{2,1,0:T(8,128)(2,1)S(1)}) %tuple.27), branch_computations={%region_0.0_spmd, %region_1.0_spmd} | conditional | bytes 3145736 | solution.py:309
  23.0 2.3 %pack.1 = bf16[128,48,128]{2,1,0:T(8,128)(2,1)S(1)} custom-call(s32[4,128]{1,0:T(4,128)S(1)} %get-tuple-element.6.ids_ref, bf16[128,512]{1,0:T(8,128)(2,1)S(1)} %get-tuple-element.48.dy_ref, bf16[4,32,512]{2,1,0:T(8,128)(2,1)S(1)} %get-tuple-element.8.x_ref), custom_call_target="tpu_custom_call" | custom-call | tf_op jit(solution)/shard_map/cond/branch_1_fun/pack/pallas_call | solution.py:239
  25.3 60.3 %all_to_all.24 = bf16[128,48,128]{2,1,0:T(8,128)(2,1)S(1)} all-to-all(bf16[128,48,128]{2,1,0:T(8,128)(2,1)S(1)} %pack.1), channel_id=1, replica_groups=mesh['dp'=4,'node'=16,'expert'=8] {'node','expert'}, dimensions={0} | all-to-all | bytes 3145728 | tf_op jit(solution)/shard_map/cond/branch_1_fun/all_to_all | solution.py:298
  85.6 2.2 %unpack.1 = (bf16[4,96,1024]{2,1,0:T(8,128)(2,1)}, bf16[96,4096]{1,0:T(8,128)(2,1)}) custom-call(bf16[16,8,48,128]{3,2,1,0:T(8,128)(2,1)S(1)} %bitcast.11), custom_call_target="tpu_custom_call" | custom-call | tf_op jit(solution)/shard_map/cond/branch_1_fun/unpack/pallas_call | solution.py:239
  88.7 3.5 %all-to-all-start.2 = ((bf16[4,96,1024]{2,1,0:T(8,128)(2,1)}), bf16[4,96,1024]{2,1,0:T(8,128)(2,1)S(1)}, u32[]{:S(2)}, u32[]{:S(2)}) async-start(bf16[4,96,1024]{2,1,0:T(8,128)(2,1)} %get-tuple-element.39), calls=%async_computation.2 | async-start | bytes 1572864 | tf_op jit(solution)/shard_map/all_to_all | solution.py:313
  92.2 1.1 slice.6
  93.2 2.3 %slice.7 = bf16[128,4096]{1,0:T(8,128)(2,1)} slice(bf16[256,5120]{1,0:T(8,128)(2,1)} %collective-permute-done.1.right), slice={[128:256], [0:4096]} | slice | bytes 2097152 | tf_op jit(solution)/shard_map/slice | solution.py:312
  95.5 4.5 %collective-permute-start.4 = (bf16[128,4096]{1,0:T(8,128)(2,1)}, bf16[128,4096]{1,0:T(8,128)(2,1)}, u32[]{:S(2)}, u32[]{:S(2)}) collective-permute-start(bf16[128,4096]{1,0:T(8,128)(2,1)} %slice.7), channel_id=1, source_target_pairs={{0,384},{128,0},{256,128},{384,256},{1,385},{129,1},{257,129},{385... | collective-permute-start | bytes 3145736 | tf_op jit(solution)/shard_map/ppermute | solution.py:312
  100.1 1.9 collective-permute-start.3
  105.0 2.7 %hidden.1 = bf16[4,4,96,256]{3,2,1,0:T(8,128)(2,1)S(1)} custom-call(s32[1]{0:T(128)} %bitcast.1.me_ref, bf16[4,96,1024]{2,1,0:T(8,128)(2,1)S(1)} %all-to-all-done.2.dy_ref, bf16[256,1024]{1,0:T(8,128)(2,1)S(1)} %copy-done.2, bf16[256,5120]{1,0:T(8,128)(2,1)S(1)} %collective-permute-done.left, bf16[256,1024]{1,0:T(8,128)(2,1)S(1)} %copy-done.4, ...), custom_call_target="tpu_custom_call" | custom-call | tf_op jit(solution)/shard_map/hidden/pallas_call | solution.py:239
  108.6 3.6 %all-to-all-start.3 = ((bf16[4,4,96,256]{3,2,1,0:T(8,128)(2,1)}), bf16[4,4,96,256]{3,2,1,0:T(8,128)(2,1)S(1)}, u32[]{:S(2)}, u32[]{:S(2)}) async-start(bf16[4,4,96,256]{3,2,1,0:T(8,128)(2,1)} %copy-done.1), calls=%async_computation.3 | async-start | bytes 1572864 | tf_op jit(solution)/shard_map/all_to_all | solution.py:321
  112.3 11.7 %collective-permute-done.4.far_high = bf16[128,4096]{1,0:T(8,128)(2,1)} collective-permute-done((bf16[128,4096]{1,0:T(8,128)(2,1)}, bf16[128,4096]{1,0:T(8,128)(2,1)}, u32[]{:S(2)}, u32[]{:S(2)}) %collective-permute-start.4) | collective-permute-done | bytes 1048608 | tf_op jit(solution)/shard_map/ppermute | solution.py:312
  124.0 2.1 %collective-permute-done.3.far_low = bf16[128,4096]{1,0:T(8,128)(2,1)} collective-permute-done((bf16[128,4096]{1,0:T(8,128)(2,1)}, bf16[128,4096]{1,0:T(8,128)(2,1)}, u32[]{:S(2)}, u32[]{:S(2)}) %collective-permute-start.3) | collective-permute-done | bytes 1048608 | tf_op jit(solution)/shard_map/ppermute | solution.py:311
  126.1 7.1 %all-to-all-done.3.part_ref = bf16[4,4,96,256]{3,2,1,0:T(8,128)(2,1)S(1)} async-done(((bf16[4,4,96,256]{3,2,1,0:T(8,128)(2,1)}), bf16[4,4,96,256]{3,2,1,0:T(8,128)(2,1)S(1)}, u32[]{:S(2)}, u32[]{:S(2)}) %all-to-all-start.3) | async-done | bytes 786464 | tf_op jit(solution)/shard_map/all_to_all | solution.py:321
  133.2 1.6 copy-done
  134.8 7.3 %backward.1 = bf16[16,8,32,128]{3,2,1,0:T(8,128)(2,1)S(1)} custom-call(s32[1]{0:T(128)} %bitcast.1.me_ref, bf16[4,4,96,256]{3,2,1,0:T(8,128)(2,1)S(1)} %all-to-all-done.3.part_ref, bf16[96,4096]{1,0:T(8,128)(2,1)} %get-tuple-element.44.x_ref, bf16[256,4096]{1,0:T(8,128)(2,1)S(1)} %bitcast.10, bf16[256,5120]{1,0:T(8,128)(2,1)S(1)} %collective-permute-done.left, ...), custom_call_target="tpu_custom_call" | custom-call | tf_op jit(solution)/shard_map/backward/pallas_call | solution.py:239
  142.1 49.8 %all_to_all.25.got_ref = bf16[128,32,128]{2,1,0:T(8,128)(2,1)S(1)} all-to-all(bf16[128,32,128]{2,1,0:T(8,128)(2,1)S(1)} %bitcast.12), channel_id=1, replica_groups=mesh['dp'=4,'node'=16,'expert'=8] {'node','expert'}, dimensions={0} | all-to-all | bytes 2097152 | tf_op jit(solution)/shard_map/all_to_all | solution.py:329
  191.9 1.9 combine.1
  (20 shorter events, 4.7 us)
Async XLA Ops:
  2.6 20.4 %copy-start.6 = (bf16[128,512]{1,0:T(8,128)(2,1)S(1)}, bf16[128,512]{1,0:T(8,128)(2,1)}, u32[]{:S(2)}) copy-start(bf16[128,512]{1,0:T(8,128)(2,1)} %param.13) | copy-start | bytes 393220
  2.6 20.4 %copy-start.7 = (s32[128,4]{0,1:T(4,128)S(1)}, s32[128,4]{0,1:T(4,128)}, u32[]{:S(2)}) copy-start(s32[128,4]{0,1:T(4,128)} %param.11) | copy-start | bytes 6148
  2.7 10.2 %all-to-all-start.1 = ((bf16[4,32,512]{2,1,0:T(8,128)(2,1)}), bf16[4,32,512]{2,1,0:T(8,128)(2,1)S(1)}, u32[]{:S(2)}, u32[]{:S(2)}) async-start(bf16[4,32,512]{2,1,0:T(8,128)(2,1)} %get-tuple-element.29.after_ref), calls=%async_computation.1 | async-start | bytes 262144 | tf_op jit(solution)/shard_map/all_to_all | solution.py:276
  12.8 75.8 %collective-permute-start = (bf16[256,5120]{1,0:T(8,128)(2,1)}, bf16[256,5120]{1,0:T(8,128)(2,1)S(1)}, u32[]{:S(2)}, u32[]{:S(2)}) collective-permute-start(bf16[256,5120]{1,0:T(8,128)(2,1)} %get-tuple-element.36), channel_id=1, source_target_pairs={{0,128},{128,256},{256,384},{384,0},{1,129},{129,257},{257,385},{3... | collective-permute-start | bytes 7864328 | tf_op jit(solution)/shard_map/ppermute | solution.py:287
  16.2 72.5 %collective-permute-start.1 = (bf16[256,5120]{1,0:T(8,128)(2,1)}, bf16[256,5120]{1,0:T(8,128)(2,1)}, u32[]{:S(2)}, u32[]{:S(2)}) collective-permute-start(bf16[256,5120]{1,0:T(8,128)(2,1)} %get-tuple-element.37), channel_id=1, source_target_pairs={{0,384},{128,0},{256,128},{384,256},{1,385},{129,1},{257,129},{385... | collective-permute-start | bytes 7864328 | tf_op jit(solution)/shard_map/ppermute | solution.py:288
  19.3 68.5 %collective-permute-start.2 = (bf16[256,1024]{1,0:T(8,128)(2,1)}, bf16[256,1024]{1,0:T(8,128)(2,1)S(1)}, u32[]{:S(2)}, u32[]{:S(2)}) collective-permute-start(bf16[256,1024]{1,0:T(8,128)(2,1)} %get-tuple-element.38), channel_id=1, source_target_pairs={{0,256},{128,384},{256,0},{384,128},{1,257},{129,385},{257,1},{385... | collective-permute-start | bytes 1572872 | tf_op jit(solution)/shard_map/ppermute | solution.py:275
  87.8 0.8 copy-start.3
  88.7 14.3 %all-to-all-start.2 = ((bf16[4,96,1024]{2,1,0:T(8,128)(2,1)}), bf16[4,96,1024]{2,1,0:T(8,128)(2,1)S(1)}, u32[]{:S(2)}, u32[]{:S(2)}) async-start(bf16[4,96,1024]{2,1,0:T(8,128)(2,1)} %get-tuple-element.39), calls=%async_computation.2 | async-start | bytes 1572864 | tf_op jit(solution)/shard_map/all_to_all | solution.py:313
  95.5 28.5 %collective-permute-start.4 = (bf16[128,4096]{1,0:T(8,128)(2,1)}, bf16[128,4096]{1,0:T(8,128)(2,1)}, u32[]{:S(2)}, u32[]{:S(2)}) collective-permute-start(bf16[128,4096]{1,0:T(8,128)(2,1)} %slice.7), channel_id=1, source_target_pairs={{0,384},{128,0},{256,128},{384,256},{1,385},{129,1},{257,129},{385... | collective-permute-start | bytes 3145736 | tf_op jit(solution)/shard_map/ppermute | solution.py:312
  100.1 26.0 %collective-permute-start.3 = (bf16[128,4096]{1,0:T(8,128)(2,1)}, bf16[128,4096]{1,0:T(8,128)(2,1)}, u32[]{:S(2)}, u32[]{:S(2)}) collective-permute-start(bf16[128,4096]{1,0:T(8,128)(2,1)} %slice.6), channel_id=1, source_target_pairs={{0,128},{128,256},{256,384},{384,0},{1,129},{129,257},{257,385},{3... | collective-permute-start | bytes 3145736 | tf_op jit(solution)/shard_map/ppermute | solution.py:311
  102.9 1.0 copy-start.2
  104.0 1.0 copy-start.4
  107.8 0.9 copy-start.1
  108.6 83.2 %copy-start.5 = (f32[128,4]{0,1:T(4,128)S(1)}, f32[128,4]{0,1:T(4,128)}, u32[]{:S(2)}) copy-start(f32[128,4]{0,1:T(4,128)} %param.12) | copy-start | bytes 6148
  108.6 24.5 %all-to-all-start.3 = ((bf16[4,4,96,256]{3,2,1,0:T(8,128)(2,1)}), bf16[4,4,96,256]{3,2,1,0:T(8,128)(2,1)S(1)}, u32[]{:S(2)}, u32[]{:S(2)}) async-start(bf16[4,4,96,256]{3,2,1,0:T(8,128)(2,1)} %copy-done.1), calls=%async_computation.3 | async-start | bytes 1572864 | tf_op jit(solution)/shard_map/all_to_all | solution.py:321
  133.2 1.6 copy-start

commit v5 on v4

--- a/solution.py
+++ b/solution.py
@@ -145,6 +145,10 @@
                         dy_ref[pair, rows, col:col + LANE] = value
                     else:
                         x_ref[rows, pair * 1024 + col:pair * 1024 + col + LANE] = value
+
+
+def halves_kernel(left, right, low_ref, high_ref, sems):
+    load(((left.at[:128, :4096], low_ref), (right.at[128:, :4096], high_ref)), sems)
 
 
 def hidden_kernel(me_ref, dy_ref, own, left, far, right, out_ref):
@@ -308,8 +312,16 @@
 
     rows_dy, rows_x = lax.cond(me >= 0, exchange, nothing, ids, cotangent, arrived)
     rows_dy, rows_x, left, right, far = lax.optimization_barrier((rows_dy, rows_x, left, right, far))
-    far_low = lax.ppermute(left[:128, :4096], "dp", to_right)
-    far_high = lax.ppermute(right[128:, :4096], "dp", to_left)
+    low, high = call(
+        halves_kernel,
+        (struct((128, 4096)), struct((128, 4096))),
+        (left, right),
+        in_specs=[pl.BlockSpec(memory_space=pl.ANY)] * 2,
+        scratch=(pltpu.SemaphoreType.DMA((2,)),),
+        name="halves",
+    )
+    far_low = lax.ppermute(low, "dp", to_right)
+    far_high = lax.ppermute(high, "dp", to_left)
     rows_dy = lax.all_to_all(rows_dy, "dp", split_axis=0, concat_axis=0, tiled=True)
     part = call(
         hidden_kernel,

time: 195 us -> 193 us (0.990)
  local copies, waits for them, and re-layouts: 8.74 us -> 5.38 us
  Pallas kernels: 23.6 us -> 26.2 us
  blocking collectives: 110 us -> 108 us
    slice x2 -> x0, local copies, waits for them, and re-layouts: 3.36 us -> none  [the longest x1 2.29 us: shards(): far_high = lax.ppermute(right[128:, :4096], 'dp', to_left)]
    pallas_call x7 -> x8, Pallas kernels: 23.6 us -> 26.2 us  [call(): pl.pallas_call(kernel, out_shape=out_shape, in_specs=in_specs or [VM] * l...]
  transfers between devices with their start and end apart: 8 -> 8, of which waited for: 4 -> 3; matrix products, arithmetic and copies ran while one was open for 2% -> 0% of each run, Pallas kernels for 6% -> 8%
where the time goes in v5:
time: 193 us
  blocking collectives  108 us (56%)
  starting transfers between devices  28.8 us (15%)
  Pallas kernels  26.2 us (14%)
  waiting for transfers between devices  23.1 us (12%)
  local copies, waits for them, and re-layouts  5.38 us (3%)
    all_to_all x1, blocking collectives, exchange(): got = lax.all_to_all(send, plane, split_axis=0, concat_axis=0, tiled=True)  60.3 us
    all_to_all x1, blocking collectives, shards(): lax.all_to_all(reply.reshape(128, 32, LANE), plane, split_axis=0, concat_...  47.9 us
    pallas_call x8, Pallas kernels, call(): pl.pallas_call(kernel, out_shape=out_shape, in_specs=in_specs or [VM] * l...  26.2 us
    ppermute x1, waiting for transfers between devices, shards(): far_low = lax.ppermute(low, 'dp', to_right)  14.3 us
    all_to_all x1, waiting for transfers between devices, shards(): part = lax.all_to_all(part, 'dp', split_axis=0, concat_axis=0, tiled=True)  7.19 us
    unnamed x16, local copies, waits for them, and re-layouts  5.38 us
    all_to_all x1, starting transfers between devices, shards(): lax.all_to_all(sorted_x, 'dp', split_axis=0, concat_axis=0, tiled=True)  4.99 us
  transfers between devices with their start and end apart: 8, of which 3 were waited for; matrix products, arithmetic and copies ran while one was open for 0% of the time, Pallas kernels for 8%

profile of v5, /device:TPU:1, one launch (start us, length us, event | category | flops | bytes accessed | tf_op | source)
XLA Modules:
  0.0 192.6 jit_solution(13844036634767358228)
XLA Ops:
  0.6 2.0 %prepare.1 = (bf16[4,32,512]{2,1,0:T(8,128)(2,1)}, bf16[256,1024]{1,0:T(8,128)(2,1)}) custom-call(s32[1]{0:T(128)} %bitcast.1.me_ref, bf16[128,512]{1,0:T(8,128)(2,1)} %x_hbm.1, s32[1,128]{1,0:T(1,128)} %bitcast.18, bf16[256,4096]{1,0:T(8,128)(2,1)} %bitcast.14), custom_call_target="tpu_custom_call" | custom-call | tf_op jit(solution)/shard_map/prepare/pallas_call | solution.py:243
  2.7 5.0 %all-to-all-start.1 = ((bf16[4,32,512]{2,1,0:T(8,128)(2,1)}), bf16[4,32,512]{2,1,0:T(8,128)(2,1)S(1)}, u32[]{:S(2)}, u32[]{:S(2)}) async-start(bf16[4,32,512]{2,1,0:T(8,128)(2,1)} %get-tuple-element.31.after_ref), calls=%async_computation.1 | async-start | bytes 262144 | tf_op jit(solution)/shard_map/all_to_all | solution.py:280
  7.6 5.1 %split.1 = (bf16[256,5120]{1,0:T(8,128)(2,1)}, bf16[256,5120]{1,0:T(8,128)(2,1)}, bf16[256,1024]{1,0:T(8,128)(2,1)}) custom-call(s32[1]{0:T(128)} %bitcast.1.me_ref, bf16[256,4096]{1,0:T(8,128)(2,1)} %bitcast.9, bf16[256,4096]{1,0:T(8,128)(2,1)} %bitcast.15, bf16[4,32,512]{2,1,0:T(8,128)(2,1)} %get-tuple-element.31.after_ref), custom_call_target="tpu_custom_call" | custom-call | tf_op jit(solution)/shard_map/split/pallas_call | solution.py:243
  12.8 3.4 %collective-permute-start = (bf16[256,5120]{1,0:T(8,128)(2,1)}, bf16[256,5120]{1,0:T(8,128)(2,1)S(1)}, u32[]{:S(2)}, u32[]{:S(2)}) collective-permute-start(bf16[256,5120]{1,0:T(8,128)(2,1)} %get-tuple-element.38), channel_id=1, source_target_pairs={{0,128},{128,256},{256,384},{384,0},{1,129},{129,257},{257,385},{3... | collective-permute-start | bytes 7864328 | tf_op jit(solution)/shard_map/ppermute | solution.py:291
  16.2 3.1 %collective-permute-start.1 = (bf16[256,5120]{1,0:T(8,128)(2,1)}, bf16[256,5120]{1,0:T(8,128)(2,1)}, u32[]{:S(2)}, u32[]{:S(2)}) collective-permute-start(bf16[256,5120]{1,0:T(8,128)(2,1)} %get-tuple-element.39), channel_id=1, source_target_pairs={{0,384},{128,0},{256,128},{384,256},{1,385},{129,1},{257,129},{385... | collective-permute-start | bytes 7864328 | tf_op jit(solution)/shard_map/ppermute | solution.py:292
  19.3 3.7 %collective-permute-start.2 = (bf16[256,1024]{1,0:T(8,128)(2,1)}, bf16[256,1024]{1,0:T(8,128)(2,1)S(1)}, u32[]{:S(2)}, u32[]{:S(2)}) collective-permute-start(bf16[256,1024]{1,0:T(8,128)(2,1)} %get-tuple-element.40), channel_id=1, source_target_pairs={{0,256},{128,384},{256,0},{384,128},{1,257},{129,385},{257,1},{385... | collective-permute-start | bytes 1572872 | tf_op jit(solution)/shard_map/ppermute | solution.py:279
  23.0 64.8 %conditional.1 = ((bf16[4,96,1024]{2,1,0:T(8,128)(2,1)}, bf16[96,4096]{1,0:T(8,128)(2,1)})) conditional(s32[]{:T(128)} %convert_element_type.3, () %tuple.17, (s32[4,128]{1,0:T(4,128)S(1)}, bf16[128,512]{1,0:T(8,128)(2,1)S(1)}, bf16[4,32,512]{2,1,0:T(8,128)(2,1)S(1)}) %tuple.27), branch_computations={%region_0.0_spmd, %region_1.0_spmd} | conditional | bytes 3145736 | solution.py:313
  23.0 2.3 %pack.1 = bf16[128,48,128]{2,1,0:T(8,128)(2,1)S(1)} custom-call(s32[4,128]{1,0:T(4,128)S(1)} %get-tuple-element.6.ids_ref, bf16[128,512]{1,0:T(8,128)(2,1)S(1)} %get-tuple-element.52.dy_ref, bf16[4,32,512]{2,1,0:T(8,128)(2,1)S(1)} %get-tuple-element.8.x_ref), custom_call_target="tpu_custom_call" | custom-call | tf_op jit(solution)/shard_map/cond/branch_1_fun/pack/pallas_call | solution.py:243
  25.3 60.3 %all_to_all.24 = bf16[128,48,128]{2,1,0:T(8,128)(2,1)S(1)} all-to-all(bf16[128,48,128]{2,1,0:T(8,128)(2,1)S(1)} %pack.1), channel_id=1, replica_groups=mesh['dp'=4,'node'=16,'expert'=8] {'node','expert'}, dimensions={0} | all-to-all | bytes 3145728 | tf_op jit(solution)/shard_map/cond/branch_1_fun/all_to_all | solution.py:302
  85.6 2.2 %unpack.1 = (bf16[4,96,1024]{2,1,0:T(8,128)(2,1)}, bf16[96,4096]{1,0:T(8,128)(2,1)}) custom-call(bf16[16,8,48,128]{3,2,1,0:T(8,128)(2,1)S(1)} %bitcast.11), custom_call_target="tpu_custom_call" | custom-call | tf_op jit(solution)/shard_map/cond/branch_1_fun/unpack/pallas_call | solution.py:243
  88.6 3.5 %all-to-all-start.2 = ((bf16[4,96,1024]{2,1,0:T(8,128)(2,1)}), bf16[4,96,1024]{2,1,0:T(8,128)(2,1)S(1)}, u32[]{:S(2)}, u32[]{:S(2)}) async-start(bf16[4,96,1024]{2,1,0:T(8,128)(2,1)} %get-tuple-element.41), calls=%async_computation.2 | async-start | bytes 1572864 | tf_op jit(solution)/shard_map/all_to_all | solution.py:325
  92.1 2.7 %halves.1 = (bf16[128,4096]{1,0:T(8,128)(2,1)}, bf16[128,4096]{1,0:T(8,128)(2,1)}) custom-call(bf16[256,5120]{1,0:T(8,128)(2,1)S(1)} %collective-permute-done.left, bf16[256,5120]{1,0:T(8,128)(2,1)} %collective-permute-done.1.right), custom_call_target="tpu_custom_call" | custom-call | tf_op jit(solution)/shard_map/halves/pallas_call | solution.py:243
  94.8 3.3 %collective-permute-start.3 = (bf16[128,4096]{1,0:T(8,128)(2,1)}, bf16[128,4096]{1,0:T(8,128)(2,1)}, u32[]{:S(2)}, u32[]{:S(2)}) collective-permute-start(bf16[128,4096]{1,0:T(8,128)(2,1)} %get-tuple-element.47), channel_id=1, source_target_pairs={{0,128},{128,256},{256,384},{384,0},{1,129},{129,257},{257,385},{3... | collective-permute-start | bytes 3145736 | tf_op jit(solution)/shard_map/ppermute | solution.py:323
  98.1 3.2 %collective-permute-start.4 = (bf16[128,4096]{1,0:T(8,128)(2,1)}, bf16[128,4096]{1,0:T(8,128)(2,1)}, u32[]{:S(2)}, u32[]{:S(2)}) collective-permute-start(bf16[128,4096]{1,0:T(8,128)(2,1)} %get-tuple-element.48), channel_id=1, source_target_pairs={{0,384},{128,0},{256,128},{384,256},{1,385},{129,1},{257,129},{385... | collective-permute-start | bytes 3145736 | tf_op jit(solution)/shard_map/ppermute | solution.py:324
  101.3 1.6 all-to-all-done.2.dy_ref
  102.9 1.0 copy-done.2
  105.0 2.7 %hidden.1 = bf16[4,4,96,256]{3,2,1,0:T(8,128)(2,1)S(1)} custom-call(s32[1]{0:T(128)} %bitcast.1.me_ref, bf16[4,96,1024]{2,1,0:T(8,128)(2,1)S(1)} %all-to-all-done.2.dy_ref, bf16[256,1024]{1,0:T(8,128)(2,1)S(1)} %copy-done.2, bf16[256,5120]{1,0:T(8,128)(2,1)S(1)} %collective-permute-done.left, bf16[256,1024]{1,0:T(8,128)(2,1)S(1)} %copy-done.4, ...), custom_call_target="tpu_custom_call" | custom-call | tf_op jit(solution)/shard_map/hidden/pallas_call | solution.py:243
  108.6 3.6 %all-to-all-start.3 = ((bf16[4,4,96,256]{3,2,1,0:T(8,128)(2,1)}), bf16[4,4,96,256]{3,2,1,0:T(8,128)(2,1)S(1)}, u32[]{:S(2)}, u32[]{:S(2)}) async-start(bf16[4,4,96,256]{3,2,1,0:T(8,128)(2,1)} %copy-done.1), calls=%async_computation.3 | async-start | bytes 1572864 | tf_op jit(solution)/shard_map/all_to_all | solution.py:333
  112.3 14.3 %collective-permute-done.3.far_low = bf16[128,4096]{1,0:T(8,128)(2,1)} collective-permute-done((bf16[128,4096]{1,0:T(8,128)(2,1)}, bf16[128,4096]{1,0:T(8,128)(2,1)}, u32[]{:S(2)}, u32[]{:S(2)}) %collective-permute-start.3) | collective-permute-done | bytes 1048608 | tf_op jit(solution)/shard_map/ppermute | solution.py:323
  126.6 7.2 %all-to-all-done.3.part_ref = bf16[4,4,96,256]{3,2,1,0:T(8,128)(2,1)S(1)} async-done(((bf16[4,4,96,256]{3,2,1,0:T(8,128)(2,1)}), bf16[4,4,96,256]{3,2,1,0:T(8,128)(2,1)S(1)}, u32[]{:S(2)}, u32[]{:S(2)}) %all-to-all-start.3) | async-done | bytes 786464 | tf_op jit(solution)/shard_map/all_to_all | solution.py:333
  133.8 1.6 copy-done
  135.4 7.3 %backward.1 = bf16[16,8,32,128]{3,2,1,0:T(8,128)(2,1)S(1)} custom-call(s32[1]{0:T(128)} %bitcast.1.me_ref, bf16[4,4,96,256]{3,2,1,0:T(8,128)(2,1)S(1)} %all-to-all-done.3.part_ref, bf16[96,4096]{1,0:T(8,128)(2,1)} %get-tuple-element.46.x_ref, bf16[256,4096]{1,0:T(8,128)(2,1)S(1)} %bitcast.10, bf16[256,5120]{1,0:T(8,128)(2,1)S(1)} %collective-permute-done.left, ...), custom_call_target="tpu_custom_call" | custom-call | tf_op jit(solution)/shard_map/backward/pallas_call | solution.py:243
  142.8 47.9 %all_to_all.25.got_ref = bf16[128,32,128]{2,1,0:T(8,128)(2,1)S(1)} all-to-all(bf16[128,32,128]{2,1,0:T(8,128)(2,1)S(1)} %bitcast.12), channel_id=1, replica_groups=mesh['dp'=4,'node'=16,'expert'=8] {'node','expert'}, dimensions={0} | all-to-all | bytes 2097152 | tf_op jit(solution)/shard_map/all_to_all | solution.py:341
  190.7 1.9 combine.1
  (19 shorter events, 2.8 us)
Async XLA Ops:
  2.6 20.3 %copy-start.6 = (bf16[128,512]{1,0:T(8,128)(2,1)S(1)}, bf16[128,512]{1,0:T(8,128)(2,1)}, u32[]{:S(2)}) copy-start(bf16[128,512]{1,0:T(8,128)(2,1)} %param.13) | copy-start | bytes 393220
  2.6 20.3 %copy-start.7 = (s32[128,4]{0,1:T(4,128)S(1)}, s32[128,4]{0,1:T(4,128)}, u32[]{:S(2)}) copy-start(s32[128,4]{0,1:T(4,128)} %param.11) | copy-start | bytes 6148
  2.7 10.1 %all-to-all-start.1 = ((bf16[4,32,512]{2,1,0:T(8,128)(2,1)}), bf16[4,32,512]{2,1,0:T(8,128)(2,1)S(1)}, u32[]{:S(2)}, u32[]{:S(2)}) async-start(bf16[4,32,512]{2,1,0:T(8,128)(2,1)} %get-tuple-element.31.after_ref), calls=%async_computation.1 | async-start | bytes 262144 | tf_op jit(solution)/shard_map/all_to_all | solution.py:280
  12.8 75.8 %collective-permute-start = (bf16[256,5120]{1,0:T(8,128)(2,1)}, bf16[256,5120]{1,0:T(8,128)(2,1)S(1)}, u32[]{:S(2)}, u32[]{:S(2)}) collective-permute-start(bf16[256,5120]{1,0:T(8,128)(2,1)} %get-tuple-element.38), channel_id=1, source_target_pairs={{0,128},{128,256},{256,384},{384,0},{1,129},{129,257},{257,385},{3... | collective-permute-start | bytes 7864328 | tf_op jit(solution)/shard_map/ppermute | solution.py:291
  16.2 72.5 %collective-permute-start.1 = (bf16[256,5120]{1,0:T(8,128)(2,1)}, bf16[256,5120]{1,0:T(8,128)(2,1)}, u32[]{:S(2)}, u32[]{:S(2)}) collective-permute-start(bf16[256,5120]{1,0:T(8,128)(2,1)} %get-tuple-element.39), channel_id=1, source_target_pairs={{0,384},{128,0},{256,128},{384,256},{1,385},{129,1},{257,129},{385... | collective-permute-start | bytes 7864328 | tf_op jit(solution)/shard_map/ppermute | solution.py:292
  19.3 68.5 %collective-permute-start.2 = (bf16[256,1024]{1,0:T(8,128)(2,1)}, bf16[256,1024]{1,0:T(8,128)(2,1)S(1)}, u32[]{:S(2)}, u32[]{:S(2)}) collective-permute-start(bf16[256,1024]{1,0:T(8,128)(2,1)} %get-tuple-element.40), channel_id=1, source_target_pairs={{0,256},{128,384},{256,0},{384,128},{1,257},{129,385},{257,1},{385... | collective-permute-start | bytes 1572872 | tf_op jit(solution)/shard_map/ppermute | solution.py:279
  87.8 0.8 copy-start.3
  88.6 14.3 %all-to-all-start.2 = ((bf16[4,96,1024]{2,1,0:T(8,128)(2,1)}), bf16[4,96,1024]{2,1,0:T(8,128)(2,1)S(1)}, u32[]{:S(2)}, u32[]{:S(2)}) async-start(bf16[4,96,1024]{2,1,0:T(8,128)(2,1)} %get-tuple-element.41), calls=%async_computation.2 | async-start | bytes 1572864 | tf_op jit(solution)/shard_map/all_to_all | solution.py:325
  94.8 31.8 %collective-permute-start.3 = (bf16[128,4096]{1,0:T(8,128)(2,1)}, bf16[128,4096]{1,0:T(8,128)(2,1)}, u32[]{:S(2)}, u32[]{:S(2)}) collective-permute-start(bf16[128,4096]{1,0:T(8,128)(2,1)} %get-tuple-element.47), channel_id=1, source_target_pairs={{0,128},{128,256},{256,384},{384,0},{1,129},{129,257},{257,385},{3... | collective-permute-start | bytes 3145736 | tf_op jit(solution)/shard_map/ppermute | solution.py:323
  98.1 28.5 %collective-permute-start.4 = (bf16[128,4096]{1,0:T(8,128)(2,1)}, bf16[128,4096]{1,0:T(8,128)(2,1)}, u32[]{:S(2)}, u32[]{:S(2)}) collective-permute-start(bf16[128,4096]{1,0:T(8,128)(2,1)} %get-tuple-element.48), channel_id=1, source_target_pairs={{0,384},{128,0},{256,128},{384,256},{1,385},{129,1},{257,129},{385... | collective-permute-start | bytes 3145736 | tf_op jit(solution)/shard_map/ppermute | solution.py:324
  102.9 1.0 copy-start.2
  104.0 1.0 copy-start.4
  107.8 0.9 copy-start.1
  108.6 82.1 %copy-start.5 = (f32[128,4]{0,1:T(4,128)S(1)}, f32[128,4]{0,1:T(4,128)}, u32[]{:S(2)}) copy-start(f32[128,4]{0,1:T(4,128)} %param.12) | copy-start | bytes 6148
  108.6 25.2 %all-to-all-start.3 = ((bf16[4,4,96,256]{3,2,1,0:T(8,128)(2,1)}), bf16[4,4,96,256]{3,2,1,0:T(8,128)(2,1)S(1)}, u32[]{:S(2)}, u32[]{:S(2)}) async-start(bf16[4,4,96,256]{3,2,1,0:T(8,128)(2,1)} %copy-done.1), calls=%async_computation.3 | async-start | bytes 1572864 | tf_op jit(solution)/shard_map/all_to_all | solution.py:333
  133.8 1.6 copy-start
